TPU v7x, 256 devices: a whole 4x4x8 slice. The times are simulated.
256 devices in a mesh: owner: 64 (over x, z_hi, y, core), qgrp: 4 (over z_lo).
Axes of the slice: x: 4, y: 4, z: 8 (z_hi: 2, z_lo: 4; z = z_hi * 4 + z_lo), core: 2. Of those that a mesh axis runs over, the one named last changes fastest.
Arguments:
- queries: float32 [3, 65536], P(None, ('owner', 'qgrp')), may hold values from -1.03 to 1.03, as said below
- winding_in: float32 [65536], P(('owner', 'qgrp')), may hold values from -2 to 2
- triangles: float32 [9, 1048576], P(None, ('owner', 'qgrp')), may hold values from -1.1 to 1.1, as said below
- dipoles: float32 [6, 8192], P(None, ('owner', 'qgrp')), may hold values from -1.2 to 1.2
- plan: int32 [4], replicated, may hold values from 0 to 63, as said below
- near_blocks: int32 [512, 16, 4], P(('owner', 'qgrp')), may hold values from 0 to 31, as said below
- near_count: int32 [512, 16], P(('owner', 'qgrp')), may hold values from 0 to 4, as said below
Outputs:
- winding_out: float32 [65536], P(('owner', 'qgrp'))
Inputs may be any that keep to these rules, and one draw needn't show every extreme that they name: `queries`: every point lies 0.004 or more away from the plane z = 0 in z. `triangles`: every corner lies within 0.001 of the plane z = 0 in z. `plan`: distinct owner indices. `near_blocks`: the entries of one list are distinct block numbers. Only the leading near_count entries of a list are live; the first tile has all 4 live for some window panel.
All inputs are finite; a program needn't handle non-finite values.
Results may differ from a plain program's by a relative error of at most 0.0003.
Values sent between devices are 32-bit elements; how exact they have to be, the bound alone decides.
A program may use at most 64 MiB of HBM per device.

v0:
```python
import jax
import jax.numpy as jnp
from jax import lax
from jax.sharding import PartitionSpec as P

TILE = 128
BLK = 128
BLOCKS = 32
NEAR = 4
TURNS = 4
PAN_TURN = 4


four_pi = 4.0 * 3.141592653589793
soften = 0.1


def broadcast(block, axis, owner):
    block = jnp.where(lax.axis_index(axis) == owner, block, jnp.zeros_like(block))
    return lax.psum(block, axis)


def inner_product(left, right):
    return left[0] * right[0] + left[1] * right[1] + left[2] * right[2]


def cross_product(left, right):
    return (
        left[1] * right[2] - left[2] * right[1],
        left[2] * right[0] - left[0] * right[2],
        left[0] * right[1] - left[1] * right[0],
    )


def solid_terms(points, corners):
    relative = [
        corners[component][None, :] - points[component % 3][:, None] for component in range(9)
    ]
    to_first = relative[0:3]
    to_second = relative[3:6]
    to_third = relative[6:9]
    length_first = jnp.sqrt(inner_product(to_first, to_first))
    length_second = jnp.sqrt(inner_product(to_second, to_second))
    length_third = jnp.sqrt(inner_product(to_third, to_third))
    volume = inner_product(to_first, cross_product(to_second, to_third))
    denominator = (
        length_first * length_second * length_third
        + inner_product(to_first, to_second) * length_third
        + inner_product(to_second, to_third) * length_first
        + inner_product(to_third, to_first) * length_second
    )
    return 2.0 * jnp.arctan2(volume, denominator) / four_pi


def dipole_terms(points, clusters):
    offset = [clusters[component][None, :] - points[component][:, None] for component in range(3)]
    normal = [clusters[3 + component][None, :] for component in range(3)]
    radius_square = inner_product(offset, offset) + soften
    return inner_product(normal, offset) / (four_pi * radius_square * jnp.sqrt(radius_square))


def on_device(queries, winding_in, triangles, dipoles, plan, near_blocks, near_count):
    tile_count = queries.shape[1] // TILE
    points = queries.reshape(3, tile_count, TILE)
    panel_rows = jnp.arange(PAN_TURN, dtype=jnp.int32)[None, :, None]
    slot_order = jnp.arange(NEAR, dtype=jnp.int32)
    total = winding_in
    group_triangles, group_dipoles = (
        lax.all_gather(triangles, "qgrp", axis=1, tiled=True),
        lax.all_gather(dipoles, "qgrp", axis=1, tiled=True),
    )
    for window_turn in range(TURNS):
        source_owner = plan[window_turn]
        all_triangles, all_dipoles = (
            broadcast(group_triangles, "owner", source_owner),
            broadcast(group_dipoles, "owner", source_owner),
        )
        corners = all_triangles.reshape(9, PAN_TURN, BLOCKS, BLK)
        centres = all_dipoles.reshape(6, PAN_TURN, BLOCKS)
        far_field = jnp.sum(dipole_terms(queries, all_dipoles), axis=1)
        first_panel = window_turn * PAN_TURN
        blocks = near_blocks[:, first_panel : first_panel + PAN_TURN, :]
        counts = near_count[:, first_panel : first_panel + PAN_TURN]
        picked = corners[:, panel_rows, blocks]
        picked_dipoles = centres[:, panel_rows, blocks]
        exact_terms = jax.vmap(solid_terms, in_axes=(1, 1))(
            points, picked.reshape(9, tile_count, -1)
        )
        exact_terms = exact_terms.reshape(tile_count, TILE, PAN_TURN, NEAR, BLK).sum(axis=4)
        dipole_part = jax.vmap(dipole_terms, in_axes=(1, 1))(
            points, picked_dipoles.reshape(6, tile_count, -1)
        )
        dipole_part = dipole_part.reshape(tile_count, TILE, PAN_TURN, NEAR)
        live_slots = slot_order[None, None, :] < counts[:, :, None]
        near_field = jnp.sum(
            jnp.where(live_slots[:, None], exact_terms - dipole_part, 0.0), axis=(2, 3)
        )
        total = total + far_field + near_field.reshape(-1)
    return total


def solution(mesh):
    return jax.shard_map(
        on_device,
        mesh=mesh,
        in_specs=(
            P(None, ("owner", "qgrp")),
            P(("owner", "qgrp")),
            P(None, ("owner", "qgrp")),
            P(None, ("owner", "qgrp")),
            P(),
            P(("owner", "qgrp"), None, None),
            P(("owner", "qgrp"), None),
        ),
        out_specs=P(("owner", "qgrp")),
        check_vma=False,
    )
```

profile of v0, /device:TPU:1, one launch (start us, length us, event | category | flops | bytes accessed | tf_op | source)
XLA Modules:
  0.0 890.5 jit_solution(10676935403331904187)
XLA Ops:
  6.5 1.4 fusion.189
  10.5 22.2 %all_gather.7 = f32[9,16384]{1,0:T(8,128)S(1)} all-gather(f32[9,4096]{1,0:T(8,128)} %param.9), channel_id=1, replica_groups=mesh['owner'=64,'qgrp'=4] {'qgrp'}, dimensions={1}, use_global_device_ids=true | all-gather | bytes 737280 | tf_op jit(solution)/shard_map/all_gather | solution.py:69
  32.7 0.3 broadcast_select_fusion.2
  33.0 0.2 copy.96
  33.3 1.4 copy.77
  34.6 0.2 copy.97
  34.9 1.3 copy.82
  36.2 0.2 copy.98
  36.5 1.3 copy.87
  37.8 0.2 copy.99
  38.1 1.4 copy.92
  39.5 0.7 copy-done
  40.5 10.7 %all-gather = f32[4,32,6]{1,2,0:T(8,128)S(1)} all-gather(f32[1,32,6]{1,2,0:T(8,128)S(1)} %bitcast.325), channel_id=1, replica_groups=mesh['owner'=64,'qgrp'=4] {'qgrp'}, dimensions={0}, use_global_device_ids=true | all-gather | bytes 3840 | tf_op jit(solution)/shard_map/all_gather | solution.py:70
  51.8 400.0 %all-reduce = (f32[6,128]{1,0:T(8,128)S(1)}, f32[6,128]{1,0:T(8,128)S(1)}, f32[6,128]{1,0:T(8,128)S(1)}, f32[6,128]{1,0:T(8,128)S(1)}) all-reduce(f32[6,128]{1,0:T(8,128)S(1)} %bitcast.300, f32[6,128]{1,0:T(8,128)S(1)} %bitcast.297, f32[6,128]{1,0:T(8,128)S(1)} %bitcast.298, ...), channel_id=1, replica_groups=mesh['owner'=64,'qgrp'=4] {'owner'}, use_global_device_ids=true, to_apply=%region_10.11 | all-reduce | flops 3072 | bytes 24576 | tf_op jit(solution)/shard_map/psum | solution.py:20
  451.9 0.7 gather_fusion.1
  452.9 0.7 gather_fusion.3
  454.1 0.7 gather_fusion.7
  455.1 0.7 gather_fusion.5
  456.0 0.4 fusion.141
  456.4 0.4 fusion.143
  457.1 380.9 %all-reduce.4.cloned.1.call-done = (f32[9,4,32,128]{3,0,2,1:T(8,128)}, f32[9,4,32,128]{3,0,2,1:T(8,128)}, f32[9,4,32,128]{3,0,2,1:T(8,128)}, f32[9,4,32,128]{3,0,2,1:T(8,128)}) async-done(((f32[9,4,32,128]{3,0,2,1:T(8,128)}, f32[9,4,32,128]{3,0,2,1:T(8,128)}, f32[9,4,32,128]{3,0,2,1:T(8,128)}, f32[9,4,32,128]{3,0,2,1:T(8,128)}), (f32[9,4,32,128]{3,0,2,1:T(8,128)}, f32[9,4,32,128]{3,0,2,1:T(8,128)}, ...) | async-done | bytes 2359312 | tf_op jit(solution)/shard_map/psum | solution.py:20
  838.1 1.8 gather_fusion.2
  840.0 1.8 gather_fusion
  842.0 1.8 gather_fusion.6
  844.0 1.8 gather_fusion.4
  845.9 9.1 %fusion.12 = f32[2,128,4,4]{1,3,2,0:T(4,128)S(1)} fusion(f32[2,4,4,128]{3,2,1,0:T(4,128)S(1)} %bitcast.262, f32[2,4,4,128]{3,2,1,0:T(4,128)S(1)} %bitcast.263, f32[2,4,4,128]{3,2,1,0:T(4,128)S(1)} %bitcast.264, f32[2,4,4,128]{3,2,1,0:T(4,128)S(1)} %bitcast.265, f32[2,4,4,128]{3,2,1,0:T(4,128)S(1)} %bitcast.266, f32[2,4,4,128]{3,2,1,0:T(4,128)S(1)} %bitcast.267, ...), kind=kLoop, calls=%fused_computation.128 | loop fusion | flops 32501760 | bytes 166912 | tf_op jit(solution)/shard_map/reduce_sum | solution.py:89
  855.0 9.3 %fusion.4 = f32[2,128,4,4]{1,3,2,0:T(4,128)S(1)} fusion(f32[2,4,4,128]{3,2,1,0:T(4,128)S(1)} %bitcast.271, f32[2,4,4,128]{3,2,1,0:T(4,128)S(1)} %bitcast.272, f32[2,4,4,128]{3,2,1,0:T(4,128)S(1)} %bitcast.273, f32[2,4,4,128]{3,2,1,0:T(4,128)S(1)} %bitcast.274, f32[2,4,4,128]{3,2,1,0:T(4,128)S(1)} %bitcast.275, f32[2,4,4,128]{3,2,1,0:T(4,128)S(1)} %bitcast.276, ...), kind=kLoop, calls=%fused_computation.120 | loop fusion | flops 32501760 | bytes 166912 | tf_op jit(solution)/shard_map/reduce_sum | solution.py:89
  864.3 9.1 %fusion.28 = f32[2,128,4,4]{1,3,2,0:T(4,128)S(1)} fusion(f32[2,4,4,128]{3,2,1,0:T(4,128)S(1)} %bitcast.280, f32[2,4,4,128]{3,2,1,0:T(4,128)S(1)} %bitcast.281, f32[2,4,4,128]{3,2,1,0:T(4,128)S(1)} %bitcast.282, f32[2,4,4,128]{3,2,1,0:T(4,128)S(1)} %bitcast.283, f32[2,4,4,128]{3,2,1,0:T(4,128)S(1)} %bitcast.284, f32[2,4,4,128]{3,2,1,0:T(4,128)S(1)} %bitcast.285, ...), kind=kLoop, calls=%fused_computation.144 | loop fusion | flops 32501760 | bytes 166912 | tf_op jit(solution)/shard_map/reduce_sum | solution.py:89
  873.4 9.3 %fusion.20 = f32[2,128,4,4]{1,3,2,0:T(4,128)S(1)} fusion(f32[2,4,4,128]{3,2,1,0:T(4,128)S(1)} %bitcast.289, f32[2,4,4,128]{3,2,1,0:T(4,128)S(1)} %bitcast.290, f32[2,4,4,128]{3,2,1,0:T(4,128)S(1)} %bitcast.291, f32[2,4,4,128]{3,2,1,0:T(4,128)S(1)} %bitcast.292, f32[2,4,4,128]{3,2,1,0:T(4,128)S(1)} %bitcast.293, f32[2,4,4,128]{3,2,1,0:T(4,128)S(1)} %bitcast.294, ...), kind=kLoop, calls=%fused_computation.136 | loop fusion | flops 32501760 | bytes 166912 | tf_op jit(solution)/shard_map/reduce_sum | solution.py:89
  882.7 0.2 select_reduce_fusion.3
  882.9 0.2 select_reduce_fusion.1
  883.1 0.6 bitcast_add_fusion
  (57 shorter events, 3.1 us)
Async XLA Ops:
  6.5 831.5 %all-reduce.4.cloned.1.call-start = ((), (), s32[]{:S(2)}) async-start(), calls=%async_computation | async-start | bytes 8388608 | tf_op jit(solution)/shard_map/psum | solution.py:20
  39.5 0.7 copy-start
  39.5 1.0 copy-start.2
  40.2 415.8 %copy-start.3 = (f32[3,256]{1,0:T(4,128)S(1)}, f32[3,256]{1,0:T(4,128)}, u32[]{:S(2)}) copy-start(f32[3,256]{1,0:T(4,128)} %param.7) | copy-start | bytes 9220
  51.2 405.7 %copy-start.1 = (s32[2,16]{1,0:T(2,128)S(1)}, s32[2,16]{1,0:T(2,128)}, u32[]{:S(2)}) copy-start(s32[2,16]{1,0:T(2,128)} %param.13) | copy-start | bytes 388
  873.3 9.7 %copy-start.4 = (f32[256]{0:T(256)S(1)}, f32[256]{0:T(256)}, u32[]{:S(2)}) copy-start(f32[256]{0:T(256)} %param.8) | copy-start | bytes 3076
Sparse Core Ops, SparseCore 0:
  39.6 798.4 all-reduce.3
where the time goes:
time: 891 us
  blocking collectives  433 us (49%)
  waiting for transfers between devices  381 us (43%)
  other arithmetic  39.2 us (4%)
  local copies, waits for them, and re-layouts  21.3 us (2%)
  between operations  16.2 us (2%)
    psum x1, blocking collectives, broadcast(): return lax.psum(block, axis)  400 us
    psum x1, waiting for transfers between devices, broadcast(): return lax.psum(block, axis)  381 us
    reduce_sum x4, other arithmetic, on_device(): exact_terms.reshape(tile_count, TILE, PAN_TURN, NEAR, BLK).sum(axis=4)  36.7 us
    all_gather x1, blocking collectives, on_device(): lax.all_gather(triangles, 'qgrp', axis=1, tiled=True)  22.2 us
  transfers between devices with their start and end apart: 1, of which 1 were waited for; matrix products, arithmetic and copies ran while one was open for 1% of the time, Pallas kernels for 0%

commit v1 on v0

v1 whole, which is shorter than its diff:
```python
import functools

import jax
import jax.numpy as jnp
from jax import lax
from jax.experimental import pallas as pl
from jax.experimental.pallas import tpu as pltpu
from jax.sharding import PartitionSpec as P

TILE = 128
BLK = 128
BLOCKS = 32
NEAR = 4
TURNS = 4
PAN_TURN = 4
PANELS = TURNS * PAN_TURN
OWNERS = 64
HALF = 5

MESH = pl.DeviceIdType.MESH

pi = 3.141592653589793
four_pi = 4.0 * pi
soften = 0.1

ATAN = (
    1.0,
    -0.3333309292793274,
    0.19993053376674652,
    -0.14207133650779724,
    0.10654675215482712,
    -0.07533672451972961,
    0.04303932562470436,
    -0.016282981261610985,
    0.0029035459738224745,
)


def gather_kernel(
    plan_ref, queries_ref, triangles_ref, dipoles_ref, lists_ref,
    panel_ref, points_ref, live_ref,
    stage, arrived, chosen, final, message, messages,
    send_one, recv_one, send_two, recv_two, send_msg, recv_msg,
):
    me = lax.axis_index("owner")
    lane = lax.axis_index("qgrp")
    group = me // TURNS
    turn = me % TURNS
    member = turn * PAN_TURN + lane

    barrier = pltpu.get_barrier_semaphore()

    def greet_owner(step, carry):
        other = (me + step) % OWNERS
        pl.semaphore_signal(barrier, inc=1, device_id=(other, lane), device_id_type=MESH)
        return carry

    def greet_member(step, carry):
        other = (lane + 1 + step // TURNS) % PAN_TURN
        pl.semaphore_signal(
            barrier, inc=1, device_id=(group * TURNS + step % TURNS, other), device_id_type=MESH
        )
        return carry

    lax.fori_loop(1, OWNERS, greet_owner, 0)
    lax.fori_loop(0, TURNS * (PAN_TURN - 1), greet_member, 0)

    for block in range(BLOCKS):
        cols = pl.ds(block * BLK, BLK)
        stage[2 * block] = triangles_ref[0:HALF, cols]
        stage[2 * block + 1, 0 : HALF - 1] = triangles_ref[HALF:9, cols]
        stage[2 * block + 1, HALF - 1 : HALF] = jnp.zeros((1, BLK), jnp.float32)
    for component in range(6):
        stage[2 * component + 1, HALF - 1 : HALF, 0:BLOCKS] = dipoles_ref[component : component + 1, :]
    message[0:3] = queries_ref[:, 0:TILE]
    message[3:6] = queries_ref[:, TILE : 2 * TILE]
    message[6:8] = lists_ref[...]

    pl.semaphore_wait(barrier, OWNERS - 1 + TURNS * (PAN_TURN - 1))

    def first_copy(other):
        return pltpu.make_async_remote_copy(
            src_ref=stage.at[other], dst_ref=arrived.at[me], send_sem=send_one, recv_sem=recv_one,
            device_id=(other, lane), device_id_type=MESH,
        )

    def send_first(step, carry):
        first_copy((me + step) % OWNERS).start()
        return carry

    lax.fori_loop(1, OWNERS, send_first, 0)

    def message_copy(to_turn, to_lane):
        return pltpu.make_async_remote_copy(
            src_ref=message, dst_ref=messages.at[member], send_sem=send_msg, recv_sem=recv_msg,
            device_id=(group * TURNS + to_turn, to_lane), device_id_type=MESH,
        )

    def send_message(step, carry):
        to = (member + step) % PANELS
        message_copy(to // PAN_TURN, to % PAN_TURN).start()
        return carry

    lax.fori_loop(1, PANELS, send_message, 0)
    messages[member] = message[...]
    arrived[me] = stage[me]

    def wait_bytes(ref, count, sem):
        part = ref.at[pl.ds(0, count)]
        pltpu.make_async_copy(part, part, sem).wait()

    wait_bytes(arrived, OWNERS - 1, recv_one)
    for window_turn in range(TURNS):
        chosen[window_turn] = arrived[plan_ref[window_turn]]

    def second_copy(other):
        return pltpu.make_async_remote_copy(
            src_ref=chosen.at[other % TURNS], dst_ref=final.at[me], send_sem=send_two, recv_sem=recv_two,
            device_id=(other, lane), device_id_type=MESH,
        )

    def send_second(step, carry):
        second_copy((me + step) % OWNERS).start()
        return carry

    lax.fori_loop(1, OWNERS, send_second, 0)
    final[me] = chosen[turn]

    wait_bytes(messages, PANELS - 1, recv_msg)
    points_ref[...] = messages[...]
    live_ref[...] = messages[:, 6:8, :].astype(jnp.int32)
    wait_bytes(final, OWNERS - 1, recv_two)
    for block in range(BLOCKS):
        panel_ref[block, 0:HALF] = final[2 * block]
        panel_ref[block, HALF : 2 * HALF] = final[2 * block + 1]
    wait_bytes(stage, OWNERS - 1, send_one)
    wait_bytes(messages, PANELS - 1, send_msg)
    wait_bytes(final, OWNERS - 1, send_two)


def near_kernel(live_ref, panel_ref, points_ref, out_ref, columns, spread, centres, real, imag, turns):
    column = (lax.axis_index("owner") % TURNS) * PAN_TURN + lax.axis_index("qgrp")

    rows = jnp.concatenate(
        [panel_ref[c, 2 * HALF - 1 : 2 * HALF, :] for c in range(6)]
        + [jnp.zeros((2, BLK), jnp.float32)], axis=0
    )
    flipped = rows.T
    for component in range(6):
        value = jnp.broadcast_to(flipped[0:BLOCKS, component : component + 1], (BLOCKS, TILE))
        if component >= 3:
            value = value * (1.0 / four_pi)
        centres[component] = value
    ones = jnp.ones((8, BLK), jnp.float32)
    block_order = lax.broadcasted_iota(jnp.int32, (BLOCKS, TILE), 0)

    def exact_block(block, first):
        corner = [
            jnp.broadcast_to(panel_ref[block, c : c + 1, :], (8, BLK)) for c in range(9)
        ]
        ax, ay, az, bx, by, bz, cx, cy, cz = corner
        ux, uy, uz = bx - ax, by - ay, bz - az
        vx, vy, vz = cx - ax, cy - ay, cz - az
        wx, wy, wz = cx - bx, cy - by, cz - bz
        ux2, uy2, uz2 = ux + ux, uy + uy, uz + uz
        nx = uy2 * vz - uz2 * vy
        ny = uz2 * vx - ux2 * vz
        nz = ux2 * vy - uy2 * vx
        side_ab = ux * ux + uy * uy + uz * uz
        side_bc = wx * wx + wy * wy + wz * wz
        side_ca = vx * vx + vy * vy + vz * vz
        for part in range(TILE // 8):
            at = pl.ds(part * 8, 8)
            qx, qy, qz = spread[0, at], spread[1, at], spread[2, at]

            def from_point(x, y, z):
                x, y, z = x - qx, y - qy, z - qz
                square = x * x + y * y + z * z
                return x, y, z, square * lax.rsqrt(square)

            px, py, pz, la = from_point(ax, ay, az)
            lb = from_point(bx, by, bz)[3]
            lc = from_point(cx, cy, cz)[3]
            y = px * nx + py * ny + pz * nz
            x = (la + lb) * (lb + lc) * (lc + la) - (side_ab * lc + side_bc * la + side_ca * lb)
            if first:
                real[at], imag[at] = x, y
                turns[at] = jnp.zeros((8, BLK), jnp.float32)
            else:
                u, v = real[at], imag[at]
                below = y < 0.0
                r, i = u * x - v * y, u * y + v * x
                same = jnp.logical_not(jnp.logical_xor(v < 0.0, below))
                wrapped = jnp.logical_and(same, jnp.logical_xor(i < 0.0, below))
                turns[at] += jnp.where(wrapped, jnp.where(below, -1.0, 1.0), 0.0)
                real[at], imag[at] = r, i

    def angle(x, y):
        ax, ay = jnp.abs(x), jnp.abs(y)
        t = jnp.minimum(ax, ay) / jnp.maximum(ax, ay)
        square = t * t
        value = jnp.full_like(t, ATAN[-1])
        for coefficient in ATAN[-2::-1]:
            value = value * square + coefficient
        value = value * t
        value = jnp.where(ay > ax, 0.5 * pi - value, value)
        value = jnp.where(x < 0.0, pi - value, value)
        return jnp.where(y < 0.0, -value, value)

    def one_member(member, carry):
        block_of_points = points_ref[member]
        columns[...] = block_of_points.T
        for half in range(2):
            count = live_ref[member, half, PANELS * NEAR + column]
            picks = [live_ref[member, half, column * NEAR + s] for s in range(NEAR)]

            offset = [
                centres[c] - jnp.broadcast_to(block_of_points[3 * half + c : 3 * half + c + 1, :], (BLOCKS, TILE))
                for c in range(3)
            ]
            square = offset[0] * offset[0] + offset[1] * offset[1] + offset[2] * offset[2] + soften
            inverse = lax.rsqrt(square)
            dipole = (centres[3] * offset[0] + centres[4] * offset[1] + centres[5] * offset[2]) * (
                inverse * inverse * inverse
            )
            for s in range(NEAR):
                pick = jnp.where(s < count, picks[s], -1)
                dipole = jnp.where(block_order == pick, 0.0, dipole)
            far = jnp.sum(dipole, axis=0, keepdims=True)
            out_ref[member, half : half + 1, :] = far

            @pl.when(count > 0)
            def _():
                for c in range(3):
                    spread[c] = jnp.broadcast_to(
                        columns[:, 3 * half + c : 3 * half + c + 1], (TILE, BLK)
                    )
                exact_block(picks[0], True)

                def more(slot, carry):
                    exact_block(live_ref[member, half, column * NEAR + slot], False)
                    return carry

                lax.fori_loop(1, count, more, 0)
                total = angle(real[...], imag[...]) * (0.5 / pi) + turns[...]
                summed = lax.dot_general(
                    ones, total, (((1,), (1,)), ((), ())),
                    precision=lax.Precision.HIGHEST, preferred_element_type=jnp.float32,
                )
                out_ref[member, half : half + 1, :] += summed[0:1]

        return carry

    lax.fori_loop(0, PANELS, one_member, 0)


def reduce_kernel(partial_ref, winding_ref, out_ref, arrived, send_sem, recv_sem):
    me = lax.axis_index("owner")
    lane = lax.axis_index("qgrp")
    group = me // TURNS
    member = (me % TURNS) * PAN_TURN + lane
    barrier = pltpu.get_barrier_semaphore()

    def device(step):
        to = (member + step) % PANELS
        return to, (group * TURNS + to // PAN_TURN, to % PAN_TURN)

    def greet(step, carry):
        pl.semaphore_signal(barrier, inc=1, device_id=device(step)[1], device_id_type=MESH)
        return carry

    lax.fori_loop(1, PANELS, greet, 0)
    pl.semaphore_wait(barrier, PANELS - 1)

    def send(step, carry):
        to, where = device(step)
        pltpu.make_async_remote_copy(
            src_ref=partial_ref.at[to], dst_ref=arrived.at[member], send_sem=send_sem, recv_sem=recv_sem,
            device_id=where, device_id_type=MESH,
        ).start()
        return carry

    lax.fori_loop(1, PANELS, send, 0)
    arrived[member] = partial_ref[member]
    part = arrived.at[pl.ds(0, PANELS - 1)]
    pltpu.make_async_copy(part, part, recv_sem).wait()
    out_ref[...] = winding_ref[...] + jnp.sum(arrived[...], axis=0)
    pltpu.make_async_copy(part, part, send_sem).wait()


def on_device(queries, winding_in, triangles, dipoles, plan, near_blocks, near_count):
    lists = jnp.concatenate(
        [near_blocks.reshape(2, PANELS * NEAR), near_count, jnp.zeros((2, 128 - PANELS * (NEAR + 1)), jnp.int32)],
        axis=1,
    ).astype(jnp.float32)
    vmem = pl.BlockSpec(memory_space=pltpu.VMEM)
    smem = pl.BlockSpec(memory_space=pltpu.SMEM)
    f32 = jnp.float32
    panel, points, live = pl.pallas_call(
        gather_kernel,
        out_shape=(
            jax.ShapeDtypeStruct((BLOCKS, 2 * HALF, BLK), f32),
            jax.ShapeDtypeStruct((PANELS, 8, TILE), f32),
            jax.ShapeDtypeStruct((PANELS, 2, 128), jnp.int32),
        ),
        in_specs=[smem, vmem, vmem, vmem, vmem],
        out_specs=(vmem, vmem, vmem),
        scratch_shapes=[
            pltpu.VMEM((OWNERS, HALF, BLK), f32),
            pltpu.VMEM((OWNERS, HALF, BLK), f32),
            pltpu.VMEM((TURNS, HALF, BLK), f32),
            pltpu.VMEM((OWNERS, HALF, BLK), f32),
            pltpu.VMEM((8, TILE), f32),
            pltpu.VMEM((PANELS, 8, TILE), f32),
        ]
        + [pltpu.SemaphoreType.DMA] * 6,
        compiler_params=pltpu.CompilerParams(collective_id=0, has_side_effects=True),
        name="gather",
    )(plan, queries, triangles, dipoles, lists)
    partial = pl.pallas_call(
        near_kernel,
        out_shape=jax.ShapeDtypeStruct((PANELS, 2, TILE), f32),
        in_specs=[smem, vmem, vmem],
        out_specs=vmem,
        scratch_shapes=[
            pltpu.VMEM((TILE, 8), f32),
            pltpu.VMEM((3, TILE, BLK), f32),
            pltpu.VMEM((6, BLOCKS, TILE), f32),
            pltpu.VMEM((TILE, BLK), f32),
            pltpu.VMEM((TILE, BLK), f32),
            pltpu.VMEM((TILE, BLK), f32),
        ],
        name="near",
    )(live, panel, points)
    total = pl.pallas_call(
        reduce_kernel,
        out_shape=jax.ShapeDtypeStruct((2, TILE), f32),
        in_specs=[vmem, vmem],
        out_specs=vmem,
        scratch_shapes=[pltpu.VMEM((PANELS, 2, TILE), f32)] + [pltpu.SemaphoreType.DMA] * 2,
        compiler_params=pltpu.CompilerParams(collective_id=1, has_side_effects=True),
        name="reduce",
    )(partial, winding_in.reshape(2, TILE))
    return total.reshape(-1)


def solution(mesh):
    return jax.shard_map(
        on_device,
        mesh=mesh,
        in_specs=(
            P(None, ("owner", "qgrp")),
            P(("owner", "qgrp")),
            P(None, ("owner", "qgrp")),
            P(None, ("owner", "qgrp")),
            P(),
            P(("owner", "qgrp"), None, None),
            P(("owner", "qgrp"), None),
        ),
        out_specs=P(("owner", "qgrp")),
        check_vma=False,
    )
```

time: 891 us -> 56.3 us (0.06)
  blocking collectives: 433 us -> 0 us
  waiting for transfers between devices: 381 us -> 0 us
  Pallas kernels: 0 us -> 52.3 us
  other arithmetic: 39.2 us -> 0.64 us
  local copies, waits for them, and re-layouts: 21.3 us -> 2.64 us
  between operations: 16.2 us -> 0.03 us
    psum x1 -> x0, blocking collectives: 400 us -> none  [broadcast(): return lax.psum(block, axis)]
    psum x1 -> x0, waiting for transfers between devices: 381 us -> none  [broadcast(): return lax.psum(block, axis)]
    pallas_call x0 -> x3, Pallas kernels: none -> 52.3 us  [the longest x1 31.1 us: on_device(): pl.pallas_call(gather_kernel, out_shape=(jax.ShapeDtypeStruct((BLOCKS, 2...]
    reduce_sum x8 -> x0, other arithmetic: 38 us -> none  [the longest x4 36.7 us: on_device(): exact_terms.reshape(tile_count, TILE, PAN_TURN, NEAR, BLK).sum(axis=4)]
    all_gather x2 -> x0, blocking collectives: 32.9 us -> none  [the longest x1 22.2 us: on_device(): lax.all_gather(triangles, 'qgrp', axis=1, tiled=True)]
    gather x12 -> x0, local copies, waits for them, and re-layouts: 10.8 us -> none  [the longest x4 7.38 us: on_device(): picked = corners[:, panel_rows, blocks]]
  transfers between devices with their start and end apart: 1 -> 0, of which waited for: 1 -> 0; matrix products, arithmetic and copies ran while one was open for 1% -> 0% of each run, Pallas kernels for 0% -> 0%
where the time goes in v1:
time: 56.3 us; the launch traced here: 55.6 us
  Pallas kernels  52.3 us (93%)
  local copies, waits for them, and re-layouts  2.64 us (5%)
  other arithmetic  0.64 us (1%)
    pallas_call x1, Pallas kernels, on_device(): pl.pallas_call(gather_kernel, out_shape=(jax.ShapeDtypeStruct((BLOCKS, 2...  31.1 us
    pallas_call x1, Pallas kernels, on_device(): pl.pallas_call(reduce_kernel, out_shape=jax.ShapeDtypeStruct((2, TILE), f...  15.4 us
    pallas_call x1, Pallas kernels, on_device(): pl.pallas_call(near_kernel, out_shape=jax.ShapeDtypeStruct((PANELS, 2, TI...  5.84 us
    unnamed x8, local copies, waits for them, and re-layouts  2.48 us

profile of v1, /device:TPU:1, one launch (start us, length us, event | category | flops | bytes accessed | tf_op | source)
XLA Modules:
  0.0 55.6 jit_solution(9586198278575512781)
XLA Ops:
  0.0 0.0 copy-start
  0.0 0.1 pad.2.clone
  0.1 0.6 %copy-done = s32[2,16,4]{1,2,0:T(4,128)S(1)} copy-done((s32[2,16,4]{1,2,0:T(4,128)S(1)}, s32[2,16,4]{1,2,0:T(4,128)}, u32[]{:S(2)}) %copy-start) | copy-done | bytes 536
  0.7 0.1 copy.9
  0.8 0.0 copy-start.2
  0.8 0.1 reshape.9
  0.9 0.6 %copy-done.2 = s32[2,16]{1,0:T(2,128)S(1)} copy-done((s32[2,16]{1,0:T(2,128)S(1)}, s32[2,16]{1,0:T(2,128)}, u32[]{:S(2)}) %copy-start.2) | copy-done | bytes 152
  1.5 0.6 %add_convert_fusion.lists_ref = f32[2,128]{1,0:T(2,128)} fusion(s32[2,16]{1,0:T(2,128)S(1)} %copy-done.2, s32[2,64]{1,0:T(2,128)S(1)} %reshape.9, s32[128]{0:T(128)S(1)} %pad.2.clone), kind=kLoop, calls=%fused_computation | loop fusion | flops 768 | bytes 2176 | tf_op jit(solution)/shard_map/convert_element_type | solution.py:295
  2.1 31.1 %gather.1 = (f32[32,10,128]{2,1,0:T(8,128)}, f32[16,8,128]{2,1,0:T(8,128)}, s32[16,2,128]{2,1,0:T(2,128)}) custom-call(s32[4]{0:T(128)} %plan_ref.1, f32[3,256]{1,0:T(4,128)} %queries_ref.1, f32[9,4096]{1,0:T(8,128)} %triangles_ref.1, f32[6,32]{1,0:T(8,128)} %dipoles_ref.1, f32[2,128]{1,0:T(2,128)} %add_convert_fusion.lists_ref), custom_call_target="tpu_custom_call" | custom-call | tf_op jit(solution)/shard_map/gather/pallas_call | solution.py:299
  33.2 5.8 %near.1.partial_ref = f32[16,2,128]{2,1,0:T(2,128)} custom-call(s32[16,2,128]{2,1,0:T(2,128)} %get-tuple-element.8.live_ref, f32[32,10,128]{2,1,0:T(8,128)} %get-tuple-element.9.panel_ref, f32[16,8,128]{2,1,0:T(8,128)} %get-tuple-element.10.points_ref), custom_call_target="tpu_custom_call" | custom-call | tf_op jit(solution)/shard_map/near/pallas_call | solution.py:320
  39.0 15.4 %reduce.1 = f32[2,128]{1,0:T(2,128)} custom-call(f32[16,2,128]{2,1,0:T(2,128)} %near.1.partial_ref, f32[2,128]{1,0:T(2,128)} %bitcast.3), custom_call_target="tpu_custom_call" | custom-call | tf_op jit(solution)/shard_map/reduce/pallas_call | solution.py:335
  54.4 0.0 copy-start.1
  54.5 0.6 %copy-done.1 = f32[2,128]{1,0:T(2,128)S(1)} copy-done((f32[2,128]{1,0:T(2,128)S(1)}, f32[2,128]{1,0:T(2,128)}, u32[]{:S(2)}) %copy-start.1) | copy-done | bytes 1048
  55.1 0.6 %copy.11 = f32[256]{0:T(256)} copy(f32[256]{0:T(256)S(1)} %bitcast.2) | data formatting | bytes 2048
  (1 shorter events, 0.0 us)
Async XLA Ops:
  0.0 0.7 %copy-start = (s32[2,16,4]{1,2,0:T(4,128)S(1)}, s32[2,16,4]{1,2,0:T(4,128)}, u32[]{:S(2)}) copy-start(s32[2,16,4]{1,2,0:T(4,128)} %param.12) | copy-start | bytes 1540
  0.8 0.7 %copy-start.2 = (s32[2,16]{1,0:T(2,128)S(1)}, s32[2,16]{1,0:T(2,128)}, u32[]{:S(2)}) copy-start(s32[2,16]{1,0:T(2,128)} %param.13) | copy-start | bytes 388
  54.4 0.6 %copy-start.1 = (f32[2,128]{1,0:T(2,128)S(1)}, f32[2,128]{1,0:T(2,128)}, u32[]{:S(2)}) copy-start(f32[2,128]{1,0:T(2,128)} %reduce.1) | copy-start | bytes 3076

commit v2 on v1

v2 whole, which is shorter than its diff:
```python
import functools

import jax
import jax.numpy as jnp
from jax import lax
from jax.experimental import pallas as pl
from jax.experimental.pallas import tpu as pltpu
from jax.sharding import PartitionSpec as P

TILE = 128
BLK = 128
BLOCKS = 32
NEAR = 4
TURNS = 4
PAN_TURN = 4
PANELS = TURNS * PAN_TURN
OWNERS = 64
ROWS = 10
PARTS = 8
MEMBERS_STEP = 2

MESH = pl.DeviceIdType.MESH

pi = 3.141592653589793
four_pi = 4.0 * pi
soften = 0.1

ATAN = (
    1.0,
    -0.3333309292793274,
    0.19993053376674652,
    -0.14207133650779724,
    0.10654675215482712,
    -0.07533672451972961,
    0.04303932562470436,
    -0.016282981261610985,
    0.0029035459738224745,
)


def block_of(place):
    kind, part = place % 4, place // 4
    return kind % 2 + (part % 2) * 2 + (kind // 2) * 4 + (part // 2) * 8


def owner_of(place, half):
    return (place // 8) * 16 + half * 8 + ((place // 4) % 2) * 4 + place % 4


def gather_kernel(
    plan_ref, queries_ref, triangles_ref, dipoles_ref, blocks_ref, count_ref,
    panel_ref, points_ref, live_ref,
    queries, triangles, dipoles, blocks, count,
    stage, arrived, chosen, final, message, messages,
    load_sems, send_one, recv_one, send_two, recv_two, recv_far, send_msg, recv_msg, known, go,
):
    me = lax.axis_index("owner")
    lane = lax.axis_index("qgrp")
    half = (me // 8) % 2
    place = ((me // 16) * 2 + (me // 4) % 2) * 4 + me % 4
    kind = me % 4
    part = place // 4
    member = kind * PAN_TURN + lane
    first = half == 0
    barrier = pltpu.get_barrier_semaphore()

    loads = [
        pltpu.make_async_copy(source, target, load_sems.at[index])
        for index, (source, target) in enumerate(
            [
                (triangles_ref, triangles), (dipoles_ref, dipoles), (queries_ref, queries),
                (blocks_ref, blocks), (count_ref, count),
            ]
        )
    ]
    for load in loads:
        load.start()

    @pl.when(first)
    def _():
        def greet(step, carry):
            pl.semaphore_signal(
                barrier, inc=1, device_id=((me + step) % OWNERS, lane), device_id_type=MESH
            )
            return carry

        lax.fori_loop(1, OWNERS, greet, 0)

        def greet_member(step, carry):
            pl.semaphore_signal(
                barrier, inc=1,
                device_id=((me // 4) * 4 + step % 4, (lane + 1 + step // 4) % PAN_TURN), device_id_type=MESH,
            )
            return carry

        lax.fori_loop(0, 4 * (PAN_TURN - 1), greet_member, 0)

    loads[0].wait()
    loads[1].wait()
    flipped = jnp.concatenate(
        [jnp.concatenate([dipoles[...], jnp.zeros((2, BLOCKS), jnp.float32)], axis=0),
         jnp.zeros((8, BLK - BLOCKS), jnp.float32)], axis=1
    ).T
    for slot in range(BLOCKS):
        block = block_of(slot)
        stage[slot, 0:9] = triangles[:, block * BLK : (block + 1) * BLK]
        stage[slot, 9:10, 0:8] = flipped[block : block + 1, :]

    def first_copy(to):
        return pltpu.make_async_remote_copy(
            src_ref=stage.at[to], dst_ref=arrived.at[me], send_sem=send_one, recv_sem=recv_one,
            device_id=(owner_of(to, 0), lane), device_id_type=MESH,
        )

    def send_first(step, carry):
        first_copy((place + step) % BLOCKS).start()
        return carry

    def make_message():
        for load in loads[2:]:
            load.wait()
        message[0:3] = queries[:, 0:TILE]
        message[3:6] = queries[:, TILE : 2 * TILE]
        shape = (PANELS, BLK)
        panel = lax.broadcasted_iota(jnp.int32, shape, 0)
        column = lax.broadcasted_iota(jnp.int32, shape, 1)
        for tile in range(2):
            wide = jnp.concatenate(
                [count[tile : tile + 1, :], jnp.zeros((1, BLK - PANELS), jnp.int32)], axis=1
            ).astype(jnp.float32)
            live = jnp.sum(
                jnp.where(panel == column, jnp.broadcast_to(wide, shape), 0.0), axis=1, keepdims=True
            )
            listed = jnp.full(shape, -1.0, jnp.float32)
            for slot in range(NEAR):
                entry = blocks[tile][:, slot : slot + 1].astype(jnp.float32)
                entry = jnp.where(live > slot, entry, -1.0)
                listed = jnp.where(column % NEAR == slot, jnp.broadcast_to(entry, shape), listed)
            listed = jnp.where(column // NEAR == panel, listed + 1.0, 0.0)
            message[6 + tile : 7 + tile] = jnp.sum(listed, axis=0, keepdims=True) - 1.0

    def send_message(step, carry):
        to = (member + step) % PANELS
        pltpu.make_async_remote_copy(
            src_ref=message, dst_ref=messages.at[member], send_sem=send_msg, recv_sem=recv_msg,
            device_id=((me // 4) * 4 + to // PAN_TURN, to % PAN_TURN), device_id_type=MESH,
        ).start()
        return carry

    def send_second(step, carry):
        to = ((part + step) % PARTS) * 4 + kind
        pltpu.make_async_remote_copy(
            src_ref=chosen, dst_ref=final.at[part], send_sem=send_two, recv_sem=recv_two,
            device_id=(owner_of(to, half), lane), device_id_type=MESH,
        ).start()
        return carry

    def wait_bytes(part, sem):
        pltpu.make_async_copy(part, part, sem).wait()

    @pl.when(first)
    def _():
        pl.semaphore_wait(barrier, BLOCKS - 1 + 4 * (PAN_TURN - 1))
        lax.fori_loop(1, BLOCKS, send_first, 0)
        make_message()
        lax.fori_loop(1, PANELS, send_message, 0)
        arrived[me] = stage[place]
        wait_bytes(arrived.at[pl.ds(0, OWNERS - 1)], recv_one)
        for turn in range(TURNS):
            chosen[turn] = arrived[plan_ref[turn]]
        lax.fori_loop(1, PARTS, send_second, 0)
        pltpu.make_async_remote_copy(
            src_ref=chosen, dst_ref=chosen, send_sem=send_two, recv_sem=recv_far,
            device_id=(me + 8, lane), device_id_type=MESH,
        ).start()
        for step in range(1, PAN_TURN):
            pl.semaphore_signal(
                known, inc=1, device_id=(me, (lane + step) % PAN_TURN), device_id_type=MESH
            )
        pl.semaphore_wait(known, PAN_TURN - 1)
        pl.semaphore_signal(go, inc=1, device_id=(me + 8, lane), device_id_type=MESH)

    @pl.when(jnp.logical_not(first))
    def _():
        pl.semaphore_wait(barrier, BLOCKS)
        lax.fori_loop(0, BLOCKS, send_first, 0)
        make_message()
        wait_bytes(chosen, recv_far)
        lax.fori_loop(1, PARTS, send_second, 0)
        pl.semaphore_wait(go, 1)
        lax.fori_loop(1, PANELS, send_message, 0)

    final[part] = chosen[...]
    messages[member] = message[...]
    wait_bytes(messages.at[pl.ds(0, PANELS - 1)], recv_msg)
    points_ref[...] = messages[...]

    shape = (PANELS, BLK)
    column = lax.broadcasted_iota(jnp.int32, shape, 1)
    before = (
        lax.broadcasted_iota(jnp.int32, (BLK, BLK), 0) < lax.broadcasted_iota(jnp.int32, (BLK, BLK), 1)
    ).astype(jnp.float32)
    for tile in range(2):
        listed = messages[:, 6 + tile, :].astype(jnp.int32)
        held = (listed % 2) + ((listed // 4) % 2) * 2 == kind
        held = jnp.logical_and(held, (column // NEAR) % PAN_TURN == lane)
        held = jnp.logical_and(held, jnp.logical_and(listed >= 0, column < PANELS * NEAR))
        value = ((listed // 2) % 2 + (listed // 8) * 2) * 4 + column // PANELS
        value = value.astype(jnp.float32)
        flags = jnp.where(held, 1.0, 0.0)
        rank = lax.dot_general(flags, before, (((1,), (0,)), ((), ())), preferred_element_type=jnp.float32)
        rank = jnp.where(held, rank, -1.0)
        packed = jnp.where(column == PANELS, jnp.sum(flags, axis=1, keepdims=True), 0.0)
        for index in range(PANELS):
            one = jnp.sum(jnp.where(jnp.abs(rank - index) < 0.5, value, 0.0), axis=1, keepdims=True)
            packed = jnp.where(column == index, one, packed)
        live_ref[:, tile, :] = packed.astype(jnp.int32)

    wait_bytes(final.at[pl.ds(0, PARTS - 1)], recv_two)
    for slot in range(BLOCKS):
        panel_ref[slot] = final[slot // 4, slot % 4]

    @pl.when(first)
    def _():
        wait_bytes(stage.at[pl.ds(0, BLOCKS - 1)], send_one)
        wait_bytes(final, send_two)

    @pl.when(jnp.logical_not(first))
    def _():
        wait_bytes(stage, send_one)
        wait_bytes(final.at[pl.ds(0, PARTS - 1)], send_two)

    wait_bytes(messages.at[pl.ds(0, PANELS - 1)], send_msg)


def near_kernel(
    live_ref, panel_ref, points_ref, out_ref, spread, centres, flipped, real, imag, turns, tiles
):
    rows = jnp.concatenate([panel_ref[slot, 9:10, :] for slot in range(BLOCKS)], axis=0)
    for component in range(6):
        value = jnp.broadcast_to(rows[:, component : component + 1], (BLOCKS, TILE))
        if component >= 3:
            value = value * (1.0 / four_pi)
        centres[component] = value

    def dipole(centre, points):
        offset = [centre[c] - jnp.broadcast_to(points[c : c + 1, :], centre[c].shape) for c in range(3)]
        square = offset[0] * offset[0] + offset[1] * offset[1] + offset[2] * offset[2] + soften
        inverse = lax.rsqrt(square)
        return (centre[3] * offset[0] + centre[4] * offset[1] + centre[5] * offset[2]) * (
            inverse * inverse * inverse
        )

    def far_field(step, carry):
        for index in range(MEMBERS_STEP):
            member = step * MEMBERS_STEP + index
            points = points_ref[member]
            flipped[member] = points.T
            for half in range(2):
                field = dipole([centres[c] for c in range(6)], points[3 * half : 3 * half + 3])
                out_ref[member, half : half + 1, :] = jnp.sum(field, axis=0, keepdims=True)
        return carry

    lax.fori_loop(0, PANELS // MEMBERS_STEP, far_field, 0)

    def exact_block(block, tile, member, half, starts):
        corner = [
            jnp.broadcast_to(panel_ref[block, c : c + 1, :], (8, BLK)) for c in range(9)
        ]
        ax, ay, az, bx, by, bz, cx, cy, cz = corner
        ux, uy, uz = bx - ax, by - ay, bz - az
        vx, vy, vz = cx - ax, cy - ay, cz - az
        wx, wy, wz = cx - bx, cy - by, cz - bz
        ux2, uy2, uz2 = ux + ux, uy + uy, uz + uz
        nx = uy2 * vz - uz2 * vy
        ny = uz2 * vx - ux2 * vz
        nz = ux2 * vy - uy2 * vx
        side_ab = ux * ux + uy * uy + uz * uz
        side_bc = wx * wx + wy * wy + wz * wz
        side_ca = vx * vx + vy * vy + vz * vz
        for part in range(TILE // 8):
            at = pl.ds(part * 8, 8)
            if not starts:
                qx, qy, qz = spread[0, at], spread[1, at], spread[2, at]
            else:
                points = flipped[member, at, :]
                qx, qy, qz = [
                    jnp.broadcast_to(points[:, 3 * half + c : 3 * half + c + 1], (8, BLK)) for c in range(3)
                ]
                spread[0, at], spread[1, at], spread[2, at] = qx, qy, qz

            def from_point(x, y, z):
                x, y, z = x - qx, y - qy, z - qz
                square = x * x + y * y + z * z
                return x, y, z, square * lax.rsqrt(square)

            px, py, pz, la = from_point(ax, ay, az)
            lb = from_point(bx, by, bz)[3]
            lc = from_point(cx, cy, cz)[3]
            y = px * nx + py * ny + pz * nz
            x = (la + lb) * (lb + lc) * (lc + la) - (side_ab * lc + side_bc * la + side_ca * lb)
            if starts:
                real[tile, at], imag[tile, at] = x, y
                turns[tile, at] = jnp.zeros((8, BLK), jnp.float32)
            else:
                u, v = real[tile, at], imag[tile, at]
                below = y < 0.0
                r, i = u * x - v * y, u * y + v * x
                same = jnp.logical_not(jnp.logical_xor(v < 0.0, below))
                wrapped = jnp.logical_and(same, jnp.logical_xor(i < 0.0, below))
                turns[tile, at] += jnp.where(wrapped, jnp.where(below, -1.0, 1.0), 0.0)
                real[tile, at], imag[tile, at] = r, i
        row = pl.ds(block, 1)
        field = dipole([centres[c, row, :] for c in range(6)], points_ref[member, 3 * half : 3 * half + 3, :])
        out_ref[member, half : half + 1, :] -= field

    def one_member(member, found):
        for half in range(2):
            count = live_ref[member, half, PANELS]

            @pl.when(count > 0)
            def _():
                tiles[found] = member * 2 + half
                exact_block(live_ref[member, half, 0], found, member, half, True)

                def more(slot, carry):
                    @pl.when(slot % 4 == 0)
                    def _():
                        u, v = real[found], imag[found]
                        factor = 1.0 / (jnp.abs(u) + jnp.abs(v))
                        real[found], imag[found] = u * factor, v * factor

                    exact_block(live_ref[member, half, slot], found, member, half, False)
                    return carry

                lax.fori_loop(1, count, more, 0)

            found = found + jnp.where(count > 0, 1, 0)
        return found

    found = lax.fori_loop(0, PANELS, one_member, jnp.int32(0))

    def angle(x, y):
        ax, ay = jnp.abs(x), jnp.abs(y)
        t = jnp.minimum(ax, ay) / jnp.maximum(ax, ay)
        square = t * t
        value = jnp.full_like(t, ATAN[-1])
        for coefficient in ATAN[-2::-1]:
            value = value * square + coefficient
        value = value * t
        value = jnp.where(ay > ax, 0.5 * pi - value, value)
        value = jnp.where(x < 0.0, pi - value, value)
        return jnp.where(y < 0.0, -value, value)

    def add_angles(tile, carry):
        total = angle(real[tile], imag[tile]) * (0.5 / pi) + turns[tile]
        where = tiles[tile]
        row = pl.ds(where % 2, 1)
        out_ref[where // 2, row, :] += jnp.sum(total.T, axis=0, keepdims=True)
        return carry

    lax.fori_loop(0, found, add_angles, 0)


def near_call(live, panel, points):
    vmem = pl.BlockSpec(memory_space=pltpu.VMEM)
    smem = pl.BlockSpec(memory_space=pltpu.SMEM)
    return pl.pallas_call(
        near_kernel,
        out_shape=jax.ShapeDtypeStruct((PANELS, 2, TILE), jnp.float32),
        in_specs=[smem, vmem, vmem],
        out_specs=vmem,
        scratch_shapes=[
            pltpu.VMEM((3, TILE, BLK), jnp.float32),
            pltpu.VMEM((6, BLOCKS, TILE), jnp.float32),
            pltpu.VMEM((PANELS, TILE, 8), jnp.float32),
            pltpu.VMEM((2 * PANELS, TILE, BLK), jnp.float32),
            pltpu.VMEM((2 * PANELS, TILE, BLK), jnp.float32),
            pltpu.VMEM((2 * PANELS, TILE, BLK), jnp.float32),
            pltpu.SMEM((2 * PANELS,), jnp.int32),
        ],
        compiler_params=pltpu.CompilerParams(vmem_limit_bytes=32 * 1024 * 1024),
        name="near",
    )(live, panel, points)


def reduce_kernel(partial_ref, winding_ref, out_ref, arrived, send_sem, recv_sem):
    me = lax.axis_index("owner")
    lane = lax.axis_index("qgrp")
    group = me // TURNS
    member = (me % TURNS) * PAN_TURN + lane
    barrier = pltpu.get_barrier_semaphore()

    def device(step):
        to = (member + step) % PANELS
        return to, (group * TURNS + to // PAN_TURN, to % PAN_TURN)

    def greet(step, carry):
        pl.semaphore_signal(barrier, inc=1, device_id=device(step)[1], device_id_type=MESH)
        return carry

    lax.fori_loop(1, PANELS, greet, 0)
    pl.semaphore_wait(barrier, PANELS - 1)

    def send(step, carry):
        to, where = device(step)
        pltpu.make_async_remote_copy(
            src_ref=partial_ref.at[to], dst_ref=arrived.at[member], send_sem=send_sem, recv_sem=recv_sem,
            device_id=where, device_id_type=MESH,
        ).start()
        return carry

    lax.fori_loop(1, PANELS, send, 0)
    arrived[member] = partial_ref[member]
    part = arrived.at[pl.ds(0, PANELS - 1)]
    pltpu.make_async_copy(part, part, recv_sem).wait()
    out_ref[...] = winding_ref[...] + jnp.sum(arrived[...], axis=0)
    pltpu.make_async_copy(part, part, send_sem).wait()


def on_device(queries, winding_in, triangles, dipoles, plan, near_blocks, near_count):
    vmem = pl.BlockSpec(memory_space=pltpu.VMEM)
    smem = pl.BlockSpec(memory_space=pltpu.SMEM)
    hbm = pl.BlockSpec(memory_space=pl.ANY)
    f32 = jnp.float32
    panel, points, live = pl.pallas_call(
        gather_kernel,
        out_shape=(
            jax.ShapeDtypeStruct((BLOCKS, ROWS, BLK), f32),
            jax.ShapeDtypeStruct((PANELS, 8, TILE), f32),
            jax.ShapeDtypeStruct((PANELS, 2, 128), jnp.int32),
        ),
        in_specs=[smem, hbm, hbm, hbm, hbm, hbm],
        out_specs=(vmem, vmem, vmem),
        scratch_shapes=[
            pltpu.VMEM((3, 2 * TILE), f32),
            pltpu.VMEM((9, BLOCKS * BLK), f32),
            pltpu.VMEM((6, BLOCKS), f32),
            pltpu.VMEM((2, PANELS, NEAR), jnp.int32),
            pltpu.VMEM((2, PANELS), jnp.int32),
            pltpu.VMEM((BLOCKS, ROWS, BLK), f32),
            pltpu.VMEM((OWNERS, ROWS, BLK), f32),
            pltpu.VMEM((TURNS, ROWS, BLK), f32),
            pltpu.VMEM((PARTS, TURNS, ROWS, BLK), f32),
            pltpu.VMEM((8, TILE), f32),
            pltpu.VMEM((PANELS, 8, TILE), f32),
            pltpu.SemaphoreType.DMA((5,)),
        ]
        + [pltpu.SemaphoreType.DMA] * 7
        + [pltpu.SemaphoreType.REGULAR] * 2,
        compiler_params=pltpu.CompilerParams(collective_id=0, has_side_effects=True),
        name="gather",
    )(plan, queries, triangles, dipoles, near_blocks, near_count)
    partial = near_call(live, panel, points)
    total = pl.pallas_call(
        reduce_kernel,
        out_shape=jax.ShapeDtypeStruct((2, TILE), f32),
        in_specs=[vmem, vmem],
        out_specs=vmem,
        scratch_shapes=[pltpu.VMEM((PANELS, 2, TILE), f32)] + [pltpu.SemaphoreType.DMA] * 2,
        compiler_params=pltpu.CompilerParams(collective_id=1, has_side_effects=True),
        name="reduce",
    )(partial, winding_in.reshape(2, TILE))
    return total.reshape(-1)


def solution(mesh):
    return jax.shard_map(
        on_device,
        mesh=mesh,
        in_specs=(
            P(None, ("owner", "qgrp")),
            P(("owner", "qgrp")),
            P(None, ("owner", "qgrp")),
            P(None, ("owner", "qgrp")),
            P(),
            P(("owner", "qgrp"), None, None),
            P(("owner", "qgrp"), None),
        ),
        out_specs=P(("owner", "qgrp")),
        check_vma=False,
    )
```

time: 56.3 us -> 51.4 us (0.913)
  Pallas kernels: 52.3 us -> 45.3 us
  local copies, waits for them, and re-layouts: 2.64 us -> 5.7 us
  other arithmetic: 0.64 us -> 0 us
    pallas_call x2, Pallas kernels: 36.9 us -> 31.8 us  [the longest x1 25.5 us: on_device(): pl.pallas_call(gather_kernel, out_shape=(jax.ShapeDtypeStruct((BLOCKS, RO...]
    unnamed x8 -> x12, local copies, waits for them, and re-layouts: 2.48 us -> 5.7 us
    pallas_call x1, Pallas kernels: 15.4 us -> 13.5 us  [on_device(): pl.pallas_call(reduce_kernel, out_shape=jax.ShapeDtypeStruct((2, TILE), f...]
    convert_element_type x1 -> x0, other arithmetic: 0.64 us -> none  [on_device(): lists = jnp.concatenate([near_blocks.reshape(2, PANELS * NEAR), near_coun...]
where the time goes in v2:
time: 51.4 us; the launch traced here: 51 us
  Pallas kernels  45.3 us (88%)
  local copies, waits for them, and re-layouts  5.7 us (11%)
    pallas_call x1, Pallas kernels, on_device(): pl.pallas_call(gather_kernel, out_shape=(jax.ShapeDtypeStruct((BLOCKS, RO...  25.5 us
    pallas_call x1, Pallas kernels, on_device(): pl.pallas_call(reduce_kernel, out_shape=jax.ShapeDtypeStruct((2, TILE), f...  13.5 us
    pallas_call x1, Pallas kernels, near_call(): pl.pallas_call(near_kernel, out_shape=jax.ShapeDtypeStruct((PANELS, 2, TI...  6.3 us
    unnamed x12, local copies, waits for them, and re-layouts  5.7 us

profile of v2, /device:TPU:1, one launch (start us, length us, event | category | flops | bytes accessed | tf_op | source)
XLA Modules:
  0.0 51.0 jit_solution(5512638610214292136)
XLA Ops:
  0.0 1.4 %copy.8.blocks_ref = s32[2,16,4]{2,1,0:T(8,128)} copy(s32[2,16,4]{1,2,0:T(4,128)} %param.12) | data formatting | bytes 1024 | tf_op args[5]
  1.4 25.5 %gather.1 = (f32[32,10,128]{2,1,0:T(8,128)}, f32[16,8,128]{2,1,0:T(8,128)}, s32[16,2,128]{2,1,0:T(2,128)}) custom-call(s32[4]{0:T(128)} %plan_ref.1, f32[3,256]{1,0:T(4,128)} %queries_ref.1, f32[9,4096]{1,0:T(8,128)} %triangles_ref.1, f32[6,32]{1,0:T(8,128)} %dipoles_ref.1, s32[2,16,4]{2,1,0:T(8,128)} %copy.8.blocks_ref, s32[2,16]{1,0:T(2,128)} %count_ref.1), custom_call_target="tpu_custom_call" | custom-call | tf_op jit(solution)/shard_map/gather/pallas_call | solution.py:426
  26.9 0.0 copy-start
  26.9 0.9 %copy-done = f32[32,10,128]{2,1,0:T(8,128)S(1)} copy-done((f32[32,10,128]{2,1,0:T(8,128)S(1)}, f32[32,10,128]{2,1,0:T(8,128)}, u32[]{:S(2)}) %copy-start) | copy-done | bytes 163864
  27.8 0.0 copy-start.2
  27.8 0.8 %copy-done.2 = f32[16,8,128]{2,1,0:T(8,128)S(1)} copy-done((f32[16,8,128]{2,1,0:T(8,128)S(1)}, f32[16,8,128]{2,1,0:T(8,128)}, u32[]{:S(2)}) %copy-start.2) | copy-done | bytes 65560
  28.7 0.0 copy-start.3
  28.7 0.7 %copy-done.3 = s32[16,2,128]{2,1,0:T(2,128)S(1)} copy-done((s32[16,2,128]{2,1,0:T(2,128)S(1)}, s32[16,2,128]{2,1,0:T(2,128)}, u32[]{:S(2)}) %copy-start.3) | copy-done | bytes 16408
  29.4 6.3 %near.1.partial_ref = f32[16,2,128]{2,1,0:T(2,128)S(1)} custom-call(s32[16,2,128]{2,1,0:T(2,128)S(1)} %copy-done.3, f32[32,10,128]{2,1,0:T(8,128)S(1)} %copy-done, f32[16,8,128]{2,1,0:T(8,128)S(1)} %copy-done.2), custom_call_target="tpu_custom_call" | custom-call | tf_op jit(solution)/shard_map/near/pallas_call | solution.py:368
  35.7 0.0 copy-start.1
  35.7 0.6 %copy-done.1 = f32[16,2,128]{2,1,0:T(2,128)} copy-done((f32[16,2,128]{2,1,0:T(2,128)}, f32[16,2,128]{2,1,0:T(2,128)S(1)}, u32[]{:S(2)}) %copy-start.1) | copy-done | bytes 16408
  36.3 13.5 %reduce.1 = f32[2,128]{1,0:T(2,128)} custom-call(f32[16,2,128]{2,1,0:T(2,128)} %copy-done.1, f32[2,128]{1,0:T(2,128)} %bitcast.3), custom_call_target="tpu_custom_call" | custom-call | tf_op jit(solution)/shard_map/reduce/pallas_call | solution.py:455
  49.8 0.0 copy-start.4
  49.8 0.7 %copy-done.4 = f32[2,128]{1,0:T(2,128)S(1)} copy-done((f32[2,128]{1,0:T(2,128)S(1)}, f32[2,128]{1,0:T(2,128)}, u32[]{:S(2)}) %copy-start.4) | copy-done | bytes 1048
  50.5 0.6 %copy.10 = f32[256]{0:T(256)} copy(f32[256]{0:T(256)S(1)} %bitcast.2) | data formatting | bytes 2048
Async XLA Ops:
  26.9 1.0 %copy-start = (f32[32,10,128]{2,1,0:T(8,128)S(1)}, f32[32,10,128]{2,1,0:T(8,128)}, u32[]{:S(2)}) copy-start(f32[32,10,128]{2,1,0:T(8,128)} %get-tuple-element.9.panel_ref) | copy-start | bytes 491524
  27.8 0.8 %copy-start.2 = (f32[16,8,128]{2,1,0:T(8,128)S(1)}, f32[16,8,128]{2,1,0:T(8,128)}, u32[]{:S(2)}) copy-start(f32[16,8,128]{2,1,0:T(8,128)} %get-tuple-element.10.points_ref) | copy-start | bytes 196612
  28.7 0.7 %copy-start.3 = (s32[16,2,128]{2,1,0:T(2,128)S(1)}, s32[16,2,128]{2,1,0:T(2,128)}, u32[]{:S(2)}) copy-start(s32[16,2,128]{2,1,0:T(2,128)} %get-tuple-element.8.live_ref) | copy-start | bytes 49156
  35.7 0.6 %copy-start.1 = (f32[16,2,128]{2,1,0:T(2,128)}, f32[16,2,128]{2,1,0:T(2,128)S(1)}, u32[]{:S(2)}) copy-start(f32[16,2,128]{2,1,0:T(2,128)S(1)} %near.1.partial_ref) | copy-start | bytes 49156
  49.8 0.7 %copy-start.4 = (f32[2,128]{1,0:T(2,128)S(1)}, f32[2,128]{1,0:T(2,128)}, u32[]{:S(2)}) copy-start(f32[2,128]{1,0:T(2,128)} %reduce.1) | copy-start | bytes 3076

commit v3 on v2

--- a/solution.py
+++ b/solution.py
@@ -49,10 +49,10 @@
 
 def gather_kernel(
     plan_ref, queries_ref, triangles_ref, dipoles_ref, blocks_ref, count_ref,
-    panel_ref, points_ref, live_ref,
-    queries, triangles, dipoles, blocks, count,
-    stage, arrived, chosen, final, message, messages,
-    load_sems, send_one, recv_one, send_two, recv_two, recv_far, send_msg, recv_msg, known, go,
+    panel_ref, poles_ref, points_ref, live_ref,
+    queries, dipoles, blocks, count, own,
+    stage, arrived, chosen, final, message, messages, poles, live,
+    load_sems, own_sem, out_sems, send_one, recv_one, send_two, recv_two, recv_far, send_msg, recv_msg, known, go,
 ):
     me = lax.axis_index("owner")
     lane = lax.axis_index("qgrp")
@@ -68,8 +68,7 @@
         pltpu.make_async_copy(source, target, load_sems.at[index])
         for index, (source, target) in enumerate(
             [
-                (triangles_ref, triangles), (dipoles_ref, dipoles), (queries_ref, queries),
-                (blocks_ref, blocks), (count_ref, count),
+                (dipoles_ref, dipoles), (queries_ref, queries), (blocks_ref, blocks), (count_ref, count),
             ]
         )
     ]
@@ -95,49 +94,48 @@
 
         lax.fori_loop(0, 4 * (PAN_TURN - 1), greet_member, 0)
 
-    loads[0].wait()
-    loads[1].wait()
-    flipped = jnp.concatenate(
-        [jnp.concatenate([dipoles[...], jnp.zeros((2, BLOCKS), jnp.float32)], axis=0),
-         jnp.zeros((8, BLK - BLOCKS), jnp.float32)], axis=1
-    ).T
-    for slot in range(BLOCKS):
-        block = block_of(slot)
-        stage[slot, 0:9] = triangles[:, block * BLK : (block + 1) * BLK]
-        stage[slot, 9:10, 0:8] = flipped[block : block + 1, :]
-
-    def first_copy(to):
-        return pltpu.make_async_remote_copy(
-            src_ref=stage.at[to], dst_ref=arrived.at[me], send_sem=send_one, recv_sem=recv_one,
+    def block_ref(place):
+        return triangles_ref.at[:, pl.ds(pl.multiple_of(block_of(place) * BLK, BLK), BLK)]
+
+    own_block = pltpu.make_async_copy(block_ref(place), own, own_sem)
+    own_block.start()
+
+    def make_stage():
+        loads[0].wait()
+        flipped = jnp.concatenate(
+            [jnp.concatenate([dipoles[...], jnp.zeros((2, BLOCKS), jnp.float32)], axis=0),
+             jnp.zeros((8, BLK - BLOCKS), jnp.float32)], axis=1
+        ).T
+        for slot in range(BLOCKS):
+            block = block_of(slot)
+            stage[slot, :, 0:8] = flipped[block : block + 1, :]
+
+    def send_first(step, carry):
+        to = (place + step) % BLOCKS
+        pltpu.make_async_remote_copy(
+            src_ref=block_ref(to), dst_ref=arrived.at[me, pl.ds(0, 9)], send_sem=send_one, recv_sem=recv_one,
             device_id=(owner_of(to, 0), lane), device_id_type=MESH,
-        )
-
-    def send_first(step, carry):
-        first_copy((place + step) % BLOCKS).start()
+        ).start()
+        return carry
+
+    def send_dipole(step, carry):
+        to = (place + step) % BLOCKS
+        pltpu.make_async_remote_copy(
+            src_ref=stage.at[to], dst_ref=arrived.at[me, pl.ds(9, 1)], send_sem=send_one, recv_sem=recv_one,
+            device_id=(owner_of(to, 0), lane), device_id_type=MESH,
+        ).start()
         return carry
 
     def make_message():
-        for load in loads[2:]:
+        for load in loads[1:]:
             load.wait()
         message[0:3] = queries[:, 0:TILE]
         message[3:6] = queries[:, TILE : 2 * TILE]
-        shape = (PANELS, BLK)
-        panel = lax.broadcasted_iota(jnp.int32, shape, 0)
-        column = lax.broadcasted_iota(jnp.int32, shape, 1)
         for tile in range(2):
-            wide = jnp.concatenate(
-                [count[tile : tile + 1, :], jnp.zeros((1, BLK - PANELS), jnp.int32)], axis=1
-            ).astype(jnp.float32)
-            live = jnp.sum(
-                jnp.where(panel == column, jnp.broadcast_to(wide, shape), 0.0), axis=1, keepdims=True
-            )
-            listed = jnp.full(shape, -1.0, jnp.float32)
-            for slot in range(NEAR):
-                entry = blocks[tile][:, slot : slot + 1].astype(jnp.float32)
-                entry = jnp.where(live > slot, entry, -1.0)
-                listed = jnp.where(column % NEAR == slot, jnp.broadcast_to(entry, shape), listed)
-            listed = jnp.where(column // NEAR == panel, listed + 1.0, 0.0)
-            message[6 + tile : 7 + tile] = jnp.sum(listed, axis=0, keepdims=True) - 1.0
+            counted = count[tile : tile + 1, :]
+            rows = [jnp.where(counted > slot, blocks[tile, slot : slot + 1, :], -1) for slot in range(NEAR)]
+            rows.append(jnp.full((1, BLK - PANELS * NEAR), -1, jnp.int32))
+            message[6 + tile : 7 + tile] = jnp.concatenate(rows, axis=1).astype(jnp.float32)
 
     def send_message(step, carry):
         to = (member + step) % PANELS
@@ -162,9 +160,13 @@
     def _():
         pl.semaphore_wait(barrier, BLOCKS - 1 + 4 * (PAN_TURN - 1))
         lax.fori_loop(1, BLOCKS, send_first, 0)
+        make_stage()
+        lax.fori_loop(1, BLOCKS, send_dipole, 0)
         make_message()
         lax.fori_loop(1, PANELS, send_message, 0)
-        arrived[me] = stage[place]
+        own_block.wait()
+        arrived[me, 0:9] = own[...]
+        arrived[me, 9:10] = stage[place]
         wait_bytes(arrived.at[pl.ds(0, OWNERS - 1)], recv_one)
         for turn in range(TURNS):
             chosen[turn] = arrived[plan_ref[turn]]
@@ -184,6 +186,9 @@
     def _():
         pl.semaphore_wait(barrier, BLOCKS)
         lax.fori_loop(0, BLOCKS, send_first, 0)
+        make_stage()
+        lax.fori_loop(0, BLOCKS, send_dipole, 0)
+        own_block.wait()
         make_message()
         wait_bytes(chosen, recv_far)
         lax.fori_loop(1, PARTS, send_second, 0)
@@ -193,7 +198,13 @@
     final[part] = chosen[...]
     messages[member] = message[...]
     wait_bytes(messages.at[pl.ds(0, PANELS - 1)], recv_msg)
-    points_ref[...] = messages[...]
+    outs = [
+        pltpu.make_async_copy(source, target, out_sems.at[index])
+        for index, (source, target) in enumerate(
+            [(messages, points_ref), (live, live_ref), (final, panel_ref), (poles, poles_ref)]
+        )
+    ]
+    outs[0].start()
 
     shape = (PANELS, BLK)
     column = lax.broadcasted_iota(jnp.int32, shape, 1)
@@ -203,9 +214,9 @@
     for tile in range(2):
         listed = messages[:, 6 + tile, :].astype(jnp.int32)
         held = (listed % 2) + ((listed // 4) % 2) * 2 == kind
-        held = jnp.logical_and(held, (column // NEAR) % PAN_TURN == lane)
+        held = jnp.logical_and(held, column % PAN_TURN == lane)
         held = jnp.logical_and(held, jnp.logical_and(listed >= 0, column < PANELS * NEAR))
-        value = ((listed // 2) % 2 + (listed // 8) * 2) * 4 + column // PANELS
+        value = ((listed // 2) % 2 + (listed // 8) * 2) * 4 + (column % PANELS) // PAN_TURN
         value = value.astype(jnp.float32)
         flags = jnp.where(held, 1.0, 0.0)
         rank = lax.dot_general(flags, before, (((1,), (0,)), ((), ())), preferred_element_type=jnp.float32)
@@ -214,58 +225,72 @@
         for index in range(PANELS):
             one = jnp.sum(jnp.where(jnp.abs(rank - index) < 0.5, value, 0.0), axis=1, keepdims=True)
             packed = jnp.where(column == index, one, packed)
-        live_ref[:, tile, :] = packed.astype(jnp.int32)
+        live[:, tile, :] = packed.astype(jnp.int32)
+    outs[1].start()
 
     wait_bytes(final.at[pl.ds(0, PARTS - 1)], recv_two)
+    outs[2].start()
     for slot in range(BLOCKS):
-        panel_ref[slot] = final[slot // 4, slot % 4]
+        poles[slot : slot + 1] = final[slot // 4, slot % 4, 9:10, :]
+    outs[3].start()
 
     @pl.when(first)
     def _():
-        wait_bytes(stage.at[pl.ds(0, BLOCKS - 1)], send_one)
+        wait_bytes(arrived.at[pl.ds(0, BLOCKS - 1)], send_one)
         wait_bytes(final, send_two)
 
     @pl.when(jnp.logical_not(first))
     def _():
-        wait_bytes(stage, send_one)
+        wait_bytes(arrived.at[pl.ds(0, BLOCKS)], send_one)
         wait_bytes(final.at[pl.ds(0, PARTS - 1)], send_two)
 
     wait_bytes(messages.at[pl.ds(0, PANELS - 1)], send_msg)
-
-
-def near_kernel(
-    live_ref, panel_ref, points_ref, out_ref, spread, centres, flipped, real, imag, turns, tiles
-):
-    rows = jnp.concatenate([panel_ref[slot, 9:10, :] for slot in range(BLOCKS)], axis=0)
+    for out in outs:
+        out.wait()
+
+
+def dipole_field(centre, points):
+    offset = [centre[c] - jnp.broadcast_to(points[c : c + 1, :], centre[c].shape) for c in range(3)]
+    square = offset[0] * offset[0] + offset[1] * offset[1] + offset[2] * offset[2] + soften
+    inverse = lax.rsqrt(square)
+    return (centre[3] * offset[0] + centre[4] * offset[1] + centre[5] * offset[2]) * (
+        inverse * inverse * inverse
+    )
+
+
+def spread_poles(rows, centres):
     for component in range(6):
         value = jnp.broadcast_to(rows[:, component : component + 1], (BLOCKS, TILE))
         if component >= 3:
             value = value * (1.0 / four_pi)
         centres[component] = value
 
-    def dipole(centre, points):
-        offset = [centre[c] - jnp.broadcast_to(points[c : c + 1, :], centre[c].shape) for c in range(3)]
-        square = offset[0] * offset[0] + offset[1] * offset[1] + offset[2] * offset[2] + soften
-        inverse = lax.rsqrt(square)
-        return (centre[3] * offset[0] + centre[4] * offset[1] + centre[5] * offset[2]) * (
-            inverse * inverse * inverse
+
+def near_kernel(
+    live_hbm, panel_hbm, poles_hbm, points_hbm, out_ref,
+    live_ref, panel_ref, poles_ref, points_ref, spread, centres, flipped, real, imag, turns, tiles, sums, sems
+):
+    loads = [
+        pltpu.make_async_copy(source, target, sems.at[index])
+        for index, (source, target) in enumerate(
+            [(live_hbm, live_ref), (panel_hbm, panel_ref), (poles_hbm, poles_ref), (points_hbm, points_ref)]
         )
-
-    def far_field(step, carry):
-        for index in range(MEMBERS_STEP):
-            member = step * MEMBERS_STEP + index
-            points = points_ref[member]
-            flipped[member] = points.T
-            for half in range(2):
-                field = dipole([centres[c] for c in range(6)], points[3 * half : 3 * half + 3])
-                out_ref[member, half : half + 1, :] = jnp.sum(field, axis=0, keepdims=True)
-        return carry
-
-    lax.fori_loop(0, PANELS // MEMBERS_STEP, far_field, 0)
+    ]
+    for load in loads:
+        load.start()
+    out_ref[...] = jnp.zeros_like(out_ref)
+    sums[...] = jnp.zeros_like(sums)
+    loads[2].wait()
+    spread_poles(poles_ref[...], centres)
+    loads[3].wait()
+    for member in range(PANELS):
+        flipped[member] = points_ref[member].T
+    loads[0].wait()
+    loads[1].wait()
 
     def exact_block(block, tile, member, half, starts):
         corner = [
-            jnp.broadcast_to(panel_ref[block, c : c + 1, :], (8, BLK)) for c in range(9)
+            jnp.broadcast_to(panel_ref[block // 4, block % 4, c : c + 1, :], (8, BLK)) for c in range(9)
         ]
         ax, ay, az, bx, by, bz, cx, cy, cz = corner
         ux, uy, uz = bx - ax, by - ay, bz - az
@@ -311,7 +336,7 @@
                 turns[tile, at] += jnp.where(wrapped, jnp.where(below, -1.0, 1.0), 0.0)
                 real[tile, at], imag[tile, at] = r, i
         row = pl.ds(block, 1)
-        field = dipole([centres[c, row, :] for c in range(6)], points_ref[member, 3 * half : 3 * half + 3, :])
+        field = dipole_field([centres[c, row, :] for c in range(6)], points_ref[member, 3 * half : 3 * half + 3, :])
         out_ref[member, half : half + 1, :] -= field
 
     def one_member(member, found):
@@ -352,44 +377,64 @@
         value = jnp.where(x < 0.0, pi - value, value)
         return jnp.where(y < 0.0, -value, value)
 
+    lanes = lax.broadcasted_iota(jnp.int32, (TILE, BLK), 1)
+
     def add_angles(tile, carry):
         total = angle(real[tile], imag[tile]) * (0.5 / pi) + turns[tile]
-        where = tiles[tile]
-        row = pl.ds(where % 2, 1)
-        out_ref[where // 2, row, :] += jnp.sum(total.T, axis=0, keepdims=True)
+        sums[...] = jnp.where(lanes == tiles[tile], jnp.sum(total, axis=1, keepdims=True), sums[...])
         return carry
 
     lax.fori_loop(0, found, add_angles, 0)
-
-
-def near_call(live, panel, points):
-    vmem = pl.BlockSpec(memory_space=pltpu.VMEM)
-    smem = pl.BlockSpec(memory_space=pltpu.SMEM)
+    rows = sums[...].T
+    for member in range(PANELS):
+        out_ref[member] += rows[2 * member : 2 * member + 2, :]
+
+
+def near_call(live, panel, poles, points):
+    hbm = pl.BlockSpec(memory_space=pl.ANY)
+    f32 = jnp.float32
     return pl.pallas_call(
         near_kernel,
-        out_shape=jax.ShapeDtypeStruct((PANELS, 2, TILE), jnp.float32),
-        in_specs=[smem, vmem, vmem],
-        out_specs=vmem,
+        out_shape=jax.ShapeDtypeStruct((PANELS, 2, TILE), f32),
+        in_specs=[hbm] * 4,
+        out_specs=pl.BlockSpec(memory_space=pltpu.VMEM),
         scratch_shapes=[
-            pltpu.VMEM((3, TILE, BLK), jnp.float32),
-            pltpu.VMEM((6, BLOCKS, TILE), jnp.float32),
-            pltpu.VMEM((PANELS, TILE, 8), jnp.float32),
-            pltpu.VMEM((2 * PANELS, TILE, BLK), jnp.float32),
-            pltpu.VMEM((2 * PANELS, TILE, BLK), jnp.float32),
-            pltpu.VMEM((2 * PANELS, TILE, BLK), jnp.float32),
+            pltpu.SMEM((PANELS, 2, 128), jnp.int32),
+            pltpu.VMEM((PARTS, TURNS, ROWS, BLK), f32),
+            pltpu.VMEM((BLOCKS, BLK), f32),
+            pltpu.VMEM((PANELS, 8, TILE), f32),
+            pltpu.VMEM((3, TILE, BLK), f32),
+            pltpu.VMEM((6, BLOCKS, TILE), f32),
+            pltpu.VMEM((PANELS, TILE, 8), f32),
+            pltpu.VMEM((2 * PANELS, TILE, BLK), f32),
+            pltpu.VMEM((2 * PANELS, TILE, BLK), f32),
+            pltpu.VMEM((2 * PANELS, TILE, BLK), f32),
             pltpu.SMEM((2 * PANELS,), jnp.int32),
+            pltpu.VMEM((TILE, BLK), f32),
+            pltpu.SemaphoreType.DMA((4,)),
         ],
-        compiler_params=pltpu.CompilerParams(vmem_limit_bytes=32 * 1024 * 1024),
+        compiler_params=pltpu.CompilerParams(vmem_limit_bytes=60 * 1024 * 1024),
         name="near",
-    )(live, panel, points)
-
-
-def reduce_kernel(partial_ref, winding_ref, out_ref, arrived, send_sem, recv_sem):
+    )(live, panel, poles, points)
+
+
+def reduce_kernel(
+    partial_hbm, poles_hbm, points_hbm, out_ref,
+    partial, far, poles, points, centres, arrived, load_sems, send_sem, recv_sem,
+):
     me = lax.axis_index("owner")
     lane = lax.axis_index("qgrp")
     group = me // TURNS
     member = (me % TURNS) * PAN_TURN + lane
     barrier = pltpu.get_barrier_semaphore()
+    loads = [
+        pltpu.make_async_copy(source, target, load_sems.at[index])
+        for index, (source, target) in enumerate(
+            [(partial_hbm, partial), (poles_hbm, poles), (points_hbm, points)]
+        )
+    ]
+    for load in loads:
+        load.start()
 
     def device(step):
         to = (member + step) % PANELS
@@ -400,21 +445,36 @@
         return carry
 
     lax.fori_loop(1, PANELS, greet, 0)
+    for load in loads:
+        load.wait()
+    spread_poles(poles[...], centres)
+
+    def far_field(step, carry):
+        for index in range(MEMBERS_STEP):
+            one = step * MEMBERS_STEP + index
+            for half in range(2):
+                field = dipole_field([centres[c] for c in range(6)], points[one, 3 * half : 3 * half + 3, :])
+                far[one, half : half + 1, :] = partial[one, half : half + 1, :] + jnp.sum(
+                    field, axis=0, keepdims=True
+                )
+        return carry
+
+    lax.fori_loop(0, PANELS // MEMBERS_STEP, far_field, 0)
     pl.semaphore_wait(barrier, PANELS - 1)
 
     def send(step, carry):
         to, where = device(step)
         pltpu.make_async_remote_copy(
-            src_ref=partial_ref.at[to], dst_ref=arrived.at[member], send_sem=send_sem, recv_sem=recv_sem,
+            src_ref=far.at[to], dst_ref=arrived.at[member], send_sem=send_sem, recv_sem=recv_sem,
             device_id=where, device_id_type=MESH,
         ).start()
         return carry
 
     lax.fori_loop(1, PANELS, send, 0)
-    arrived[member] = partial_ref[member]
+    arrived[member] = far[member]
     part = arrived.at[pl.ds(0, PANELS - 1)]
     pltpu.make_async_copy(part, part, recv_sem).wait()
-    out_ref[...] = winding_ref[...] + jnp.sum(arrived[...], axis=0)
+    out_ref[...] = jnp.sum(arrived[...], axis=0)
     pltpu.make_async_copy(part, part, send_sem).wait()
 
 
@@ -423,45 +483,60 @@
     smem = pl.BlockSpec(memory_space=pltpu.SMEM)
     hbm = pl.BlockSpec(memory_space=pl.ANY)
     f32 = jnp.float32
-    panel, points, live = pl.pallas_call(
+    panel, poles, points, live = pl.pallas_call(
         gather_kernel,
         out_shape=(
-            jax.ShapeDtypeStruct((BLOCKS, ROWS, BLK), f32),
+            jax.ShapeDtypeStruct((PARTS, TURNS, ROWS, BLK), f32),
+            jax.ShapeDtypeStruct((BLOCKS, BLK), f32),
             jax.ShapeDtypeStruct((PANELS, 8, TILE), f32),
             jax.ShapeDtypeStruct((PANELS, 2, 128), jnp.int32),
         ),
         in_specs=[smem, hbm, hbm, hbm, hbm, hbm],
-        out_specs=(vmem, vmem, vmem),
+        out_specs=(hbm, hbm, hbm, hbm),
         scratch_shapes=[
             pltpu.VMEM((3, 2 * TILE), f32),
-            pltpu.VMEM((9, BLOCKS * BLK), f32),
             pltpu.VMEM((6, BLOCKS), f32),
-            pltpu.VMEM((2, PANELS, NEAR), jnp.int32),
+            pltpu.VMEM((2, NEAR, PANELS), jnp.int32),
             pltpu.VMEM((2, PANELS), jnp.int32),
-            pltpu.VMEM((BLOCKS, ROWS, BLK), f32),
+            pltpu.VMEM((9, BLK), f32),
+            pltpu.VMEM((BLOCKS, 1, BLK), f32),
             pltpu.VMEM((OWNERS, ROWS, BLK), f32),
             pltpu.VMEM((TURNS, ROWS, BLK), f32),
             pltpu.VMEM((PARTS, TURNS, ROWS, BLK), f32),
             pltpu.VMEM((8, TILE), f32),
             pltpu.VMEM((PANELS, 8, TILE), f32),
-            pltpu.SemaphoreType.DMA((5,)),
+            pltpu.VMEM((BLOCKS, BLK), f32),
+            pltpu.VMEM((PANELS, 2, 128), jnp.int32),
+            pltpu.SemaphoreType.DMA((4,)),
+            pltpu.SemaphoreType.DMA,
+            pltpu.SemaphoreType.DMA((4,)),
         ]
         + [pltpu.SemaphoreType.DMA] * 7
         + [pltpu.SemaphoreType.REGULAR] * 2,
         compiler_params=pltpu.CompilerParams(collective_id=0, has_side_effects=True),
         name="gather",
-    )(plan, queries, triangles, dipoles, near_blocks, near_count)
-    partial = near_call(live, panel, points)
+    )(plan, queries, triangles, dipoles, near_blocks.transpose(0, 2, 1), near_count)
+    partial = near_call(live, panel, poles, points)
     total = pl.pallas_call(
         reduce_kernel,
         out_shape=jax.ShapeDtypeStruct((2, TILE), f32),
-        in_specs=[vmem, vmem],
+        in_specs=[hbm] * 3,
         out_specs=vmem,
-        scratch_shapes=[pltpu.VMEM((PANELS, 2, TILE), f32)] + [pltpu.SemaphoreType.DMA] * 2,
+        scratch_shapes=[
+            pltpu.VMEM((PANELS, 2, TILE), f32),
+            pltpu.VMEM((PANELS, 2, TILE), f32),
+            pltpu.VMEM((BLOCKS, BLK), f32),
+            pltpu.VMEM((PANELS, 8, TILE), f32),
+            pltpu.VMEM((6, BLOCKS, TILE), f32),
+            pltpu.VMEM((PANELS, 2, TILE), f32),
+            pltpu.SemaphoreType.DMA((3,)),
+            pltpu.SemaphoreType.DMA,
+            pltpu.SemaphoreType.DMA,
+        ],
         compiler_params=pltpu.CompilerParams(collective_id=1, has_side_effects=True),
         name="reduce",
-    )(partial, winding_in.reshape(2, TILE))
-    return total.reshape(-1)
+    )(partial, poles, points)
+    return winding_in + total.reshape(-1)
 
 
 def solution(mesh):

time: 51.4 us -> 48.5 us (0.944)
  local copies, waits for them, and re-layouts: 5.7 us -> 0.01 us
  Pallas kernels: 45.3 us -> 47 us
  other arithmetic: 0 us -> 1.22 us
    unnamed x12 -> x2, local copies, waits for them, and re-layouts: 5.7 us -> 0.01 us
    pallas_call x1, Pallas kernels: 6.3 us -> 11.6 us  [near_call(): pl.pallas_call(near_kernel, out_shape=jax.ShapeDtypeStruct((PANELS, 2, TI...]
    pallas_call x1, Pallas kernels: 13.5 us -> 9.01 us  [on_device(): pl.pallas_call(reduce_kernel, out_shape=jax.ShapeDtypeStruct((2, TILE), f...]
    add x0 -> x1, other arithmetic: none -> 1.22 us  [on_device(): return winding_in + total.reshape(-1)]
    pallas_call x1, Pallas kernels: 25.5 us -> 26.4 us  [on_device(): pl.pallas_call(gather_kernel, out_shape=(jax.ShapeDtypeStruct((PARTS, TUR...]
where the time goes in v3:
time: 48.5 us; the launch traced here: 48.3 us
  Pallas kernels  47 us (97%)
  other arithmetic  1.22 us (3%)
    pallas_call x1, Pallas kernels, on_device(): pl.pallas_call(gather_kernel, out_shape=(jax.ShapeDtypeStruct((PARTS, TUR...  26.4 us
    pallas_call x1, Pallas kernels, near_call(): pl.pallas_call(near_kernel, out_shape=jax.ShapeDtypeStruct((PANELS, 2, TI...  11.6 us
    pallas_call x1, Pallas kernels, on_device(): pl.pallas_call(reduce_kernel, out_shape=jax.ShapeDtypeStruct((2, TILE), f...  9.01 us
    add x1, other arithmetic, on_device(): return winding_in + total.reshape(-1)  1.22 us

profile of v3, /device:TPU:1, one launch (start us, length us, event | category | flops | bytes accessed | tf_op | source)
XLA Modules:
  0.0 48.3 jit_solution(3096769952740999819)
XLA Ops:
  0.0 26.4 %gather.1 = (f32[8,4,10,128]{3,2,1,0:T(8,128)}, f32[32,128]{1,0:T(8,128)}, f32[16,8,128]{2,1,0:T(8,128)}, s32[16,2,128]{2,1,0:T(2,128)}) custom-call(s32[4]{0:T(128)} %plan_ref.1, f32[3,256]{1,0:T(4,128)} %queries_ref.1, f32[9,4096]{1,0:T(8,128)} %triangles_ref.1, f32[6,32]{1,0:T(8,128)} %dipoles_ref.1, s32[2,4,16]{2,1,0:T(4,128)} %bitcast.3, s32[2,16]{1,0:T(2,128)} %count_ref.1), custom_call_target="tpu_custom_call" | custom-call | tf_op jit(solution)/shard_map/gather/pallas_call | solution.py:486
  26.4 11.6 %near.1.partial_hbm = f32[16,2,128]{2,1,0:T(2,128)} custom-call(s32[16,2,128]{2,1,0:T(2,128)} %get-tuple-element.9.live_hbm, f32[8,4,10,128]{3,2,1,0:T(8,128)} %get-tuple-element.10.panel_hbm, f32[32,128]{1,0:T(8,128)} %get-tuple-element.11.poles_hbm, f32[16,8,128]{2,1,0:T(8,128)} %get-tuple-element.12.points_hbm), custom_call_target="tpu_custom_call" | custom-call | tf_op jit(solution)/shard_map/near/pallas_call | solution.py:396
  38.0 0.0 copy-start
  38.0 9.0 %reduce.1 = f32[2,128]{1,0:T(2,128)} custom-call(f32[16,2,128]{2,1,0:T(2,128)} %near.1.partial_hbm, f32[32,128]{1,0:T(8,128)} %get-tuple-element.11.poles_hbm, f32[16,8,128]{2,1,0:T(8,128)} %get-tuple-element.12.points_hbm), custom_call_target="tpu_custom_call" | custom-call | tf_op jit(solution)/shard_map/reduce/pallas_call | solution.py:520
  47.0 0.0 copy-done
  47.1 1.2 %bitcast_add_fusion = f32[256]{0:T(256)} fusion(f32[256]{0:T(256)S(1)} %copy-done, f32[2,128]{1,0:T(2,128)} %reduce.1), kind=kLoop, calls=%fused_computation | loop fusion | flops 256 | bytes 3072 | tf_op jit(solution)/shard_map/add | solution.py:539
Async XLA Ops:
  38.0 9.0 %copy-start = (f32[256]{0:T(256)S(1)}, f32[256]{0:T(256)}, u32[]{:S(2)}) copy-start(f32[256]{0:T(256)} %param.8) | copy-start | bytes 3076

commit v4 on v3

--- a/solution.py
+++ b/solution.py
@@ -26,15 +26,13 @@
 soften = 0.1
 
 ATAN = (
-    1.0,
-    -0.3333309292793274,
-    0.19993053376674652,
-    -0.14207133650779724,
-    0.10654675215482712,
-    -0.07533672451972961,
-    0.04303932562470436,
-    -0.016282981261610985,
-    0.0029035459738224745,
+    0.9999994039535522,
+    -0.3332701325416565,
+    0.19887319207191467,
+    -0.13512171804904938,
+    0.08435401320457458,
+    -0.03744291514158249,
+    0.008006880059838295,
 )
 
 
@@ -47,12 +45,16 @@
     return (place // 8) * 16 + half * 8 + ((place // 4) % 2) * 4 + place % 4
 
 
+def stage_place(slot):
+    return (slot // 8) * 8 + (slot % 2) * 4 + (slot // 2) % 4
+
+
 def gather_kernel(
     plan_ref, queries_ref, triangles_ref, dipoles_ref, blocks_ref, count_ref,
     panel_ref, poles_ref, points_ref, live_ref,
-    queries, dipoles, blocks, count, own,
-    stage, arrived, chosen, final, message, messages, poles, live,
-    load_sems, own_sem, out_sems, send_one, recv_one, send_two, recv_two, recv_far, send_msg, recv_msg, known, go,
+    queries, triangles, dipoles, blocks, count,
+    stage, arrived, gathered, picked, late, chosen, final, message, messages, poles, live,
+    load_sems, out_sems, send_one, recv_one, send_late, recv_late, send_two, recv_two, recv_far, send_msg, recv_msg, known, go,
 ):
     me = lax.axis_index("owner")
     lane = lax.axis_index("qgrp")
@@ -61,6 +63,8 @@
     kind = me % 4
     part = place // 4
     member = kind * PAN_TURN + lane
+    mirror = PAN_TURN - 1 - lane
+    role = half * lane + (1 - half) * mirror
     first = half == 0
     barrier = pltpu.get_barrier_semaphore()
 
@@ -68,66 +72,78 @@
         pltpu.make_async_copy(source, target, load_sems.at[index])
         for index, (source, target) in enumerate(
             [
-                (dipoles_ref, dipoles), (queries_ref, queries), (blocks_ref, blocks), (count_ref, count),
+                (triangles_ref, triangles), (dipoles_ref, dipoles), (queries_ref, queries),
+                (blocks_ref, blocks), (count_ref, count),
             ]
         )
     ]
     for load in loads:
         load.start()
 
+    def greet(owner, to_lane):
+        pl.semaphore_signal(barrier, inc=1, device_id=(owner, to_lane), device_id_type=MESH)
+
     @pl.when(first)
     def _():
-        def greet(step, carry):
-            pl.semaphore_signal(
-                barrier, inc=1, device_id=((me + step) % OWNERS, lane), device_id_type=MESH
-            )
+        for side in range(2):
+            greet(owner_of(place - (part % 2) * 4 + side * 4, 1), mirror)
+
+        def greet_one(step, carry):
+            greet(owner_of((place + step) % BLOCKS, 0), mirror)
             return carry
 
-        lax.fori_loop(1, OWNERS, greet, 0)
-
-        def greet_member(step, carry):
-            pl.semaphore_signal(
-                barrier, inc=1,
-                device_id=((me // 4) * 4 + step % 4, (lane + 1 + step // 4) % PAN_TURN), device_id_type=MESH,
-            )
+        lax.fori_loop(0, BLOCKS, greet_one, 0)
+        for step in range(1, PARTS):
+            greet(owner_of(((part + step) % PARTS) * 4 + kind, 0), lane)
+        for step in range(1, 4):
+            greet((me // 4) * 4 + (me + step) % 4, lane)
+        for step in range(4):
+            greet((me // 4) * 4 + step, (lane + 2) % PAN_TURN)
+            greet((me // 4) * 4 + step, PAN_TURN - 1 - (lane + 2) % PAN_TURN)
+
+    squad = (part // 2) * 4 + kind
+
+    def comrade(step):
+        other = (squad + step) % 16
+        return other, ((other // 4) * 16 + 8 + (part % 2) * 4 + other % 4, lane)
+
+    @pl.when(jnp.logical_not(first))
+    def _():
+        def greet_comrade(step, carry):
+            greet(*comrade(step)[1])
             return carry
 
-        lax.fori_loop(0, 4 * (PAN_TURN - 1), greet_member, 0)
-
-    def block_ref(place):
-        return triangles_ref.at[:, pl.ds(pl.multiple_of(block_of(place) * BLK, BLK), BLK)]
-
-    own_block = pltpu.make_async_copy(block_ref(place), own, own_sem)
-    own_block.start()
-
-    def make_stage():
-        loads[0].wait()
-        flipped = jnp.concatenate(
-            [jnp.concatenate([dipoles[...], jnp.zeros((2, BLOCKS), jnp.float32)], axis=0),
-             jnp.zeros((8, BLK - BLOCKS), jnp.float32)], axis=1
-        ).T
-        for slot in range(BLOCKS):
-            block = block_of(slot)
-            stage[slot, :, 0:8] = flipped[block : block + 1, :]
+        lax.fori_loop(1, 16, greet_comrade, 0)
+
+    loads[1].wait()
+    flipped = jnp.concatenate(
+        [jnp.concatenate([dipoles[...], jnp.zeros((2, BLOCKS), jnp.float32)], axis=0),
+         jnp.zeros((8, BLK - BLOCKS), jnp.float32)], axis=1
+    ).T
+    loads[0].wait()
+    for slot in range(BLOCKS):
+        block = block_of(stage_place(slot))
+        stage[slot // 2, slot % 2, 0:9] = triangles[:, block * BLK : (block + 1) * BLK]
+        stage[slot // 2, slot % 2, 9:10, 0:8] = flipped[block : block + 1, :]
 
     def send_first(step, carry):
         to = (place + step) % BLOCKS
         pltpu.make_async_remote_copy(
-            src_ref=block_ref(to), dst_ref=arrived.at[me, pl.ds(0, 9)], send_sem=send_one, recv_sem=recv_one,
-            device_id=(owner_of(to, 0), lane), device_id_type=MESH,
+            src_ref=stage.at[(to // 8) * 4 + to % 4, (to // 4) % 2], dst_ref=arrived.at[place], send_sem=send_one, recv_sem=recv_one,
+            device_id=(owner_of(to, 0), mirror), device_id_type=MESH,
         ).start()
         return carry
 
-    def send_dipole(step, carry):
-        to = (place + step) % BLOCKS
+    def send_comrade(step, carry):
+        other, where = comrade(step)
         pltpu.make_async_remote_copy(
-            src_ref=stage.at[to], dst_ref=arrived.at[me, pl.ds(9, 1)], send_sem=send_one, recv_sem=recv_one,
-            device_id=(owner_of(to, 0), lane), device_id_type=MESH,
+            src_ref=stage.at[other], dst_ref=gathered.at[squad], send_sem=send_one, recv_sem=recv_one,
+            device_id=where, device_id_type=MESH,
         ).start()
         return carry
 
     def make_message():
-        for load in loads[1:]:
+        for load in loads[2:]:
             load.wait()
         message[0:3] = queries[:, 0:TILE]
         message[3:6] = queries[:, TILE : 2 * TILE]
@@ -145,53 +161,60 @@
         ).start()
         return carry
 
-    def send_second(step, carry):
-        to = ((part + step) % PARTS) * 4 + kind
-        pltpu.make_async_remote_copy(
-            src_ref=chosen, dst_ref=final.at[part], send_sem=send_two, recv_sem=recv_two,
-            device_id=(owner_of(to, half), lane), device_id_type=MESH,
-        ).start()
-        return carry
+    def send_second():
+        for step in (5, 4, 3, 6, 2, 7, 1):
+            to = ((part + step) % PARTS) * 4 + kind
+            pltpu.make_async_remote_copy(
+                src_ref=chosen, dst_ref=final.at[part], send_sem=send_two, recv_sem=recv_two,
+                device_id=(owner_of(to, half), lane), device_id_type=MESH,
+            ).start()
 
     def wait_bytes(part, sem):
         pltpu.make_async_copy(part, part, sem).wait()
 
     @pl.when(first)
     def _():
-        pl.semaphore_wait(barrier, BLOCKS - 1 + 4 * (PAN_TURN - 1))
-        lax.fori_loop(1, BLOCKS, send_first, 0)
-        make_stage()
-        lax.fori_loop(1, BLOCKS, send_dipole, 0)
+        pl.semaphore_wait(barrier, BLOCKS + PARTS - 1 + 3 + 8)
+        lax.fori_loop(0, BLOCKS, send_first, 0)
         make_message()
         lax.fori_loop(1, PANELS, send_message, 0)
-        own_block.wait()
-        arrived[me, 0:9] = own[...]
-        arrived[me, 9:10] = stage[place]
-        wait_bytes(arrived.at[pl.ds(0, OWNERS - 1)], recv_one)
+        wait_bytes(arrived, recv_one)
+        wait_bytes(late, recv_late)
         for turn in range(TURNS):
-            chosen[turn] = arrived[plan_ref[turn]]
-        lax.fori_loop(1, PARTS, send_second, 0)
+            owner = plan_ref[turn]
+            early = arrived[((owner // 16) * 2 + (owner // 4) % 2) * 4 + owner % 4]
+            chosen[turn] = jnp.where((owner // 8) % 2 == 0, early, late[(owner // 4) % 2, turn])
         pltpu.make_async_remote_copy(
             src_ref=chosen, dst_ref=chosen, send_sem=send_two, recv_sem=recv_far,
-            device_id=(me + 8, lane), device_id_type=MESH,
+            device_id=(me + 8, mirror), device_id_type=MESH,
         ).start()
+        send_second()
         for step in range(1, PAN_TURN):
             pl.semaphore_signal(
                 known, inc=1, device_id=(me, (lane + step) % PAN_TURN), device_id_type=MESH
             )
         pl.semaphore_wait(known, PAN_TURN - 1)
-        pl.semaphore_signal(go, inc=1, device_id=(me + 8, lane), device_id_type=MESH)
+        pl.semaphore_signal(go, inc=1, device_id=(me + 8, mirror), device_id_type=MESH)
 
     @pl.when(jnp.logical_not(first))
     def _():
-        pl.semaphore_wait(barrier, BLOCKS)
-        lax.fori_loop(0, BLOCKS, send_first, 0)
-        make_stage()
-        lax.fori_loop(0, BLOCKS, send_dipole, 0)
-        own_block.wait()
+        pl.semaphore_wait(barrier, 15 + 2)
+        lax.fori_loop(1, 16, send_comrade, 0)
+        gathered[squad] = stage[squad]
+        wait_bytes(gathered.at[pl.ds(0, 15)], recv_one)
+        for turn in range(TURNS):
+            owner = plan_ref[turn]
+            pair = gathered[(owner // 16) * 4 + owner % 4]
+            picked[0, turn] = pair[0]
+            picked[1, turn] = pair[1]
+        for side in range(2):
+            pltpu.make_async_remote_copy(
+                src_ref=picked.at[side], dst_ref=late.at[part % 2], send_sem=send_late, recv_sem=recv_late,
+                device_id=(owner_of(place - (part % 2) * 4 + side * 4, 0), mirror), device_id_type=MESH,
+            ).start()
         make_message()
         wait_bytes(chosen, recv_far)
-        lax.fori_loop(1, PARTS, send_second, 0)
+        send_second()
         pl.semaphore_wait(go, 1)
         lax.fori_loop(1, PANELS, send_message, 0)
 
@@ -214,7 +237,7 @@
     for tile in range(2):
         listed = messages[:, 6 + tile, :].astype(jnp.int32)
         held = (listed % 2) + ((listed // 4) % 2) * 2 == kind
-        held = jnp.logical_and(held, column % PAN_TURN == lane)
+        held = jnp.logical_and(held, column % PAN_TURN == role)
         held = jnp.logical_and(held, jnp.logical_and(listed >= 0, column < PANELS * NEAR))
         value = ((listed // 2) % 2 + (listed // 8) * 2) * 4 + (column % PANELS) // PAN_TURN
         value = value.astype(jnp.float32)
@@ -236,12 +259,13 @@
 
     @pl.when(first)
     def _():
-        wait_bytes(arrived.at[pl.ds(0, BLOCKS - 1)], send_one)
+        wait_bytes(stage, send_one)
         wait_bytes(final, send_two)
 
     @pl.when(jnp.logical_not(first))
     def _():
-        wait_bytes(arrived.at[pl.ds(0, BLOCKS)], send_one)
+        wait_bytes(stage.at[pl.ds(0, 15)], send_one)
+        wait_bytes(picked, send_late)
         wait_bytes(final.at[pl.ds(0, PARTS - 1)], send_two)
 
     wait_bytes(messages.at[pl.ds(0, PANELS - 1)], send_msg)
@@ -268,27 +292,82 @@
 
 def near_kernel(
     live_hbm, panel_hbm, poles_hbm, points_hbm, out_ref,
-    live_ref, panel_ref, poles_ref, points_ref, spread, centres, flipped, real, imag, turns, tiles, sums, sems
+    live_ref, panel_ref, poles_ref, given, points_ref, flipped, picker, centres,
+    spread_0, spread_1, real_0, real_1, imag_0, imag_1, turns_0, turns_1, tiles, sums, minus, sems
 ):
+    spread, real, imag, turns = (spread_0, spread_1), (real_0, real_1), (imag_0, imag_1), (turns_0, turns_1)
     loads = [
         pltpu.make_async_copy(source, target, sems.at[index])
         for index, (source, target) in enumerate(
-            [(live_hbm, live_ref), (panel_hbm, panel_ref), (poles_hbm, poles_ref), (points_hbm, points_ref)]
+            [(live_hbm, live_ref), (panel_hbm, panel_ref), (poles_hbm, poles_ref), (points_hbm, given)]
         )
     ]
     for load in loads:
         load.start()
-    out_ref[...] = jnp.zeros_like(out_ref)
+    minus[...] = jnp.zeros_like(minus)
     sums[...] = jnp.zeros_like(sums)
+    real_0[...] = jnp.ones_like(real_0)
+    imag_0[...] = jnp.zeros_like(imag_0)
+    turns_0[...] = jnp.zeros_like(turns_0)
     loads[2].wait()
     spread_poles(poles_ref[...], centres)
     loads[3].wait()
     for member in range(PANELS):
-        flipped[member] = points_ref[member].T
+        for half in range(2):
+            points_ref[2 * member + half, 0:3] = given[member, 3 * half : 3 * half + 3]
     loads[0].wait()
-    loads[1].wait()
-
-    def exact_block(block, tile, member, half, starts):
+
+    tiles[0] = 2 * PANELS
+    found = jnp.int32(0)
+    for tile in range(2 * PANELS):
+        tiles[found + 1] = tile
+        found = found + jnp.where(live_ref[tile // 2, tile % 2, PANELS] > 0, 1, 0)
+    tiles[found + 1] = 0
+    lanes = lax.broadcasted_iota(jnp.int32, (8, BLK), 1)
+
+    for member in range(PANELS):
+        rest = given[member]
+        parts = []
+        for _ in range(3):
+            parts.append(rest.astype(jnp.bfloat16).astype(jnp.float32))
+            rest = rest - parts[-1]
+        parts.append(jnp.zeros_like(rest))
+        flipped[member] = jnp.concatenate(parts, axis=0).T.astype(jnp.bfloat16)
+    shape = (32, 3 * BLK)
+    entry = lax.broadcasted_iota(jnp.int32, shape, 0)
+    component = lax.broadcasted_iota(jnp.int32, shape, 1) // BLK
+    for half in range(2):
+        wanted = jnp.logical_and(entry % 8 == 3 * half + component, entry < 24)
+        picker[half] = jnp.where(wanted, 1.0, 0.0).astype(jnp.bfloat16)
+
+    def widen(tile):
+        return lax.dot_general(
+            flipped[tile // 2], picker[tile % 2], (((1,), (0,)), ((), ())), preferred_element_type=jnp.float32
+        )
+
+    def spread_part(place, part, wide):
+        at = pl.ds(part * 8, 8)
+        for c in range(3):
+            spread[place][c, at] = wide[part * 8 : part * 8 + 8, c * BLK : (c + 1) * BLK]
+
+    def angle(x, y):
+        ax, ay = jnp.abs(x), jnp.abs(y)
+        t = jnp.minimum(ax, ay) * pl.reciprocal(jnp.maximum(ax, ay), approx=True)
+        square = t * t
+        value = jnp.full_like(t, ATAN[-1] * 0.5 / pi)
+        for coefficient in ATAN[-2::-1]:
+            value = value * square + coefficient * 0.5 / pi
+        value = value * t
+        value = jnp.where(ay > ax, 0.25 - value, value)
+        value = jnp.where(x < 0.0, 0.5 - value, value)
+        return jnp.where(y < 0.0, -value, value)
+
+    def angle_part(place, part, tile):
+        at = pl.ds(part * 8, 8)
+        total = angle(real[place][at], imag[place][at]) + turns[place][at]
+        sums[at] = jnp.where(lanes == tile, jnp.sum(total, axis=1, keepdims=True), sums[at])
+
+    def exact_block(block, tile, place, starts, beside):
         corner = [
             jnp.broadcast_to(panel_ref[block // 4, block % 4, c : c + 1, :], (8, BLK)) for c in range(9)
         ]
@@ -305,14 +384,8 @@
         side_ca = vx * vx + vy * vy + vz * vz
         for part in range(TILE // 8):
             at = pl.ds(part * 8, 8)
-            if not starts:
-                qx, qy, qz = spread[0, at], spread[1, at], spread[2, at]
-            else:
-                points = flipped[member, at, :]
-                qx, qy, qz = [
-                    jnp.broadcast_to(points[:, 3 * half + c : 3 * half + c + 1], (8, BLK)) for c in range(3)
-                ]
-                spread[0, at], spread[1, at], spread[2, at] = qx, qy, qz
+            beside(part)
+            qx, qy, qz = spread[place][0, at], spread[place][1, at], spread[place][2, at]
 
             def from_point(x, y, z):
                 x, y, z = x - qx, y - qy, z - qz
@@ -325,69 +398,70 @@
             y = px * nx + py * ny + pz * nz
             x = (la + lb) * (lb + lc) * (lc + la) - (side_ab * lc + side_bc * la + side_ca * lb)
             if starts:
-                real[tile, at], imag[tile, at] = x, y
-                turns[tile, at] = jnp.zeros((8, BLK), jnp.float32)
+                real[place][at], imag[place][at] = x, y
+                turns[place][at] = jnp.zeros((8, BLK), jnp.float32)
             else:
-                u, v = real[tile, at], imag[tile, at]
+                u, v = real[place][at], imag[place][at]
                 below = y < 0.0
                 r, i = u * x - v * y, u * y + v * x
                 same = jnp.logical_not(jnp.logical_xor(v < 0.0, below))
                 wrapped = jnp.logical_and(same, jnp.logical_xor(i < 0.0, below))
-                turns[tile, at] += jnp.where(wrapped, jnp.where(below, -1.0, 1.0), 0.0)
-                real[tile, at], imag[tile, at] = r, i
+                turns[place][at] += jnp.where(wrapped, jnp.where(below, -1.0, 1.0), 0.0)
+                real[place][at], imag[place][at] = r, i
         row = pl.ds(block, 1)
-        field = dipole_field([centres[c, row, :] for c in range(6)], points_ref[member, 3 * half : 3 * half + 3, :])
-        out_ref[member, half : half + 1, :] -= field
-
-    def one_member(member, found):
-        for half in range(2):
-            count = live_ref[member, half, PANELS]
-
-            @pl.when(count > 0)
+        field = dipole_field([centres[c, row, :] for c in range(6)], points_ref[tile, 0:3, :])
+        minus[pl.ds(tile, 1), :] -= field
+
+    first = widen(tiles[1])
+    for part in range(TILE // 8):
+        spread_part(1, part, first)
+    loads[1].wait()
+
+    def one_tile(index, place):
+        tile = tiles[index]
+        last, following = tiles[index - 1], tiles[index + 1]
+        member, half = tile // 2, tile % 2
+        across = widen(following)
+
+        def beside(part):
+            angle_part(1 - place, part, last)
+            spread_part(1 - place, part, across)
+
+        exact_block(live_ref[member, half, 0], tile, place, True, beside)
+
+        def more(slot, carry):
+            @pl.when(slot % 4 == 0)
             def _():
-                tiles[found] = member * 2 + half
-                exact_block(live_ref[member, half, 0], found, member, half, True)
-
-                def more(slot, carry):
-                    @pl.when(slot % 4 == 0)
-                    def _():
-                        u, v = real[found], imag[found]
-                        factor = 1.0 / (jnp.abs(u) + jnp.abs(v))
-                        real[found], imag[found] = u * factor, v * factor
-
-                    exact_block(live_ref[member, half, slot], found, member, half, False)
-                    return carry
-
-                lax.fori_loop(1, count, more, 0)
-
-            found = found + jnp.where(count > 0, 1, 0)
-        return found
-
-    found = lax.fori_loop(0, PANELS, one_member, jnp.int32(0))
-
-    def angle(x, y):
-        ax, ay = jnp.abs(x), jnp.abs(y)
-        t = jnp.minimum(ax, ay) / jnp.maximum(ax, ay)
-        square = t * t
-        value = jnp.full_like(t, ATAN[-1])
-        for coefficient in ATAN[-2::-1]:
-            value = value * square + coefficient
-        value = value * t
-        value = jnp.where(ay > ax, 0.5 * pi - value, value)
-        value = jnp.where(x < 0.0, pi - value, value)
-        return jnp.where(y < 0.0, -value, value)
-
-    lanes = lax.broadcasted_iota(jnp.int32, (TILE, BLK), 1)
-
-    def add_angles(tile, carry):
-        total = angle(real[tile], imag[tile]) * (0.5 / pi) + turns[tile]
-        sums[...] = jnp.where(lanes == tiles[tile], jnp.sum(total, axis=1, keepdims=True), sums[...])
+                u, v = real[place][...], imag[place][...]
+                factor = 1.0 / (jnp.abs(u) + jnp.abs(v))
+                real[place][...], imag[place][...] = u * factor, v * factor
+
+            exact_block(live_ref[member, half, slot], tile, place, False, lambda part: None)
+            return carry
+
+        lax.fori_loop(1, live_ref[member, half, PANELS], more, 0)
+
+    def two_tiles(step, carry):
+        one_tile(2 * step + 1, 1)
+
+        @pl.when(2 * step + 2 <= found)
+        def _():
+            one_tile(2 * step + 2, 0)
+
         return carry
 
-    lax.fori_loop(0, found, add_angles, 0)
+    lax.fori_loop(0, (found + 1) // 2, two_tiles, 0)
+    for place in range(2):
+
+        @pl.when(found % 2 == place)
+        def _():
+            for part in range(TILE // 8):
+                angle_part(place, part, tiles[found])
+
     rows = sums[...].T
+    rows = rows[0 : 2 * PANELS, :] + minus[...]
     for member in range(PANELS):
-        out_ref[member] += rows[2 * member : 2 * member + 2, :]
+        out_ref[member] = rows[2 * member : 2 * member + 2, :]
 
 
 def near_call(live, panel, poles, points):
@@ -403,14 +477,18 @@
             pltpu.VMEM((PARTS, TURNS, ROWS, BLK), f32),
             pltpu.VMEM((BLOCKS, BLK), f32),
             pltpu.VMEM((PANELS, 8, TILE), f32),
+            pltpu.VMEM((2 * PANELS, 8, TILE), f32),
+            pltpu.VMEM((PANELS, TILE, 32), jnp.bfloat16),
+            pltpu.VMEM((2, 32, 3 * BLK), jnp.bfloat16),
+            pltpu.VMEM((6, BLOCKS, TILE), f32),
             pltpu.VMEM((3, TILE, BLK), f32),
-            pltpu.VMEM((6, BLOCKS, TILE), f32),
-            pltpu.VMEM((PANELS, TILE, 8), f32),
-            pltpu.VMEM((2 * PANELS, TILE, BLK), f32),
-            pltpu.VMEM((2 * PANELS, TILE, BLK), f32),
-            pltpu.VMEM((2 * PANELS, TILE, BLK), f32),
-            pltpu.SMEM((2 * PANELS,), jnp.int32),
+            pltpu.VMEM((3, TILE, BLK), f32),
+        ]
+        + [pltpu.VMEM((TILE, BLK), f32)] * 6
+        + [
+            pltpu.SMEM((2 * PANELS + 2,), jnp.int32),
             pltpu.VMEM((TILE, BLK), f32),
+            pltpu.VMEM((2 * PANELS, TILE), f32),
             pltpu.SemaphoreType.DMA((4,)),
         ],
         compiler_params=pltpu.CompilerParams(vmem_limit_bytes=60 * 1024 * 1024),
@@ -495,23 +573,25 @@
         out_specs=(hbm, hbm, hbm, hbm),
         scratch_shapes=[
             pltpu.VMEM((3, 2 * TILE), f32),
+            pltpu.VMEM((9, BLOCKS * BLK), f32),
             pltpu.VMEM((6, BLOCKS), f32),
             pltpu.VMEM((2, NEAR, PANELS), jnp.int32),
             pltpu.VMEM((2, PANELS), jnp.int32),
-            pltpu.VMEM((9, BLK), f32),
-            pltpu.VMEM((BLOCKS, 1, BLK), f32),
-            pltpu.VMEM((OWNERS, ROWS, BLK), f32),
+            pltpu.VMEM((BLOCKS // 2, 2, ROWS, BLK), f32),
+            pltpu.VMEM((BLOCKS, ROWS, BLK), f32),
+            pltpu.VMEM((BLOCKS // 2, 2, ROWS, BLK), f32),
+            pltpu.VMEM((2, TURNS, ROWS, BLK), f32),
+            pltpu.VMEM((2, TURNS, ROWS, BLK), f32),
             pltpu.VMEM((TURNS, ROWS, BLK), f32),
             pltpu.VMEM((PARTS, TURNS, ROWS, BLK), f32),
             pltpu.VMEM((8, TILE), f32),
             pltpu.VMEM((PANELS, 8, TILE), f32),
             pltpu.VMEM((BLOCKS, BLK), f32),
             pltpu.VMEM((PANELS, 2, 128), jnp.int32),
-            pltpu.SemaphoreType.DMA((4,)),
-            pltpu.SemaphoreType.DMA,
+            pltpu.SemaphoreType.DMA((5,)),
             pltpu.SemaphoreType.DMA((4,)),
         ]
-        + [pltpu.SemaphoreType.DMA] * 7
+        + [pltpu.SemaphoreType.DMA] * 9
         + [pltpu.SemaphoreType.REGULAR] * 2,
         compiler_params=pltpu.CompilerParams(collective_id=0, has_side_effects=True),
         name="gather",

time: 48.5 us -> 43 us (0.89)
  Pallas kernels: 47 us -> 41.6 us
    pallas_call x1, Pallas kernels: 11.6 us -> 7.08 us  [near_call(): pl.pallas_call(near_kernel, out_shape=jax.ShapeDtypeStruct((PANELS, 2, TI...]
    pallas_call x1, Pallas kernels: 26.4 us -> 24.9 us  [on_device(): pl.pallas_call(gather_kernel, out_shape=(jax.ShapeDtypeStruct((PARTS, TUR...]
    pallas_call x1, Pallas kernels: 9.01 us -> 9.59 us  [on_device(): pl.pallas_call(reduce_kernel, out_shape=jax.ShapeDtypeStruct((2, TILE), f...]
where the time goes in v4:
time: 43 us; the launch traced here: 42.9 us
  Pallas kernels  41.6 us (97%)
  other arithmetic  1.22 us (3%)
    pallas_call x1, Pallas kernels, on_device(): pl.pallas_call(gather_kernel, out_shape=(jax.ShapeDtypeStruct((PARTS, TUR...  24.9 us
    pallas_call x1, Pallas kernels, on_device(): pl.pallas_call(reduce_kernel, out_shape=jax.ShapeDtypeStruct((2, TILE), f...  9.59 us
    pallas_call x1, Pallas kernels, near_call(): pl.pallas_call(near_kernel, out_shape=jax.ShapeDtypeStruct((PANELS, 2, TI...  7.08 us
    add x1, other arithmetic, on_device(): return winding_in + total.reshape(-1)  1.22 us

profile of v4, /device:TPU:1, one launch (start us, length us, event | category | flops | bytes accessed | tf_op | source)
XLA Modules:
  0.0 42.9 jit_solution(6930307223358505848)
XLA Ops:
  0.0 24.9 %gather.1 = (f32[8,4,10,128]{3,2,1,0:T(8,128)}, f32[32,128]{1,0:T(8,128)}, f32[16,8,128]{2,1,0:T(8,128)}, s32[16,2,128]{2,1,0:T(2,128)}) custom-call(s32[4]{0:T(128)} %plan_ref.1, f32[3,256]{1,0:T(4,128)} %queries_ref.1, f32[9,4096]{1,0:T(8,128)} %triangles_ref.1, f32[6,32]{1,0:T(8,128)} %dipoles_ref.1, s32[2,4,16]{2,1,0:T(4,128)} %bitcast.3, s32[2,16]{1,0:T(2,128)} %count_ref.1), custom_call_target="tpu_custom_call" | custom-call | tf_op jit(solution)/shard_map/gather/pallas_call | solution.py:564
  24.9 7.1 %near.1.partial_hbm = f32[16,2,128]{2,1,0:T(2,128)} custom-call(s32[16,2,128]{2,1,0:T(2,128)} %get-tuple-element.9.live_hbm, f32[8,4,10,128]{3,2,1,0:T(8,128)} %get-tuple-element.10.panel_hbm, f32[32,128]{1,0:T(8,128)} %get-tuple-element.11.poles_hbm, f32[16,8,128]{2,1,0:T(8,128)} %get-tuple-element.12.points_hbm), custom_call_target="tpu_custom_call" | custom-call | tf_op jit(solution)/shard_map/near/pallas_call | solution.py:470
  32.0 0.0 copy-start
  32.0 9.6 %reduce.1 = f32[2,128]{1,0:T(2,128)} custom-call(f32[16,2,128]{2,1,0:T(2,128)} %near.1.partial_hbm, f32[32,128]{1,0:T(8,128)} %get-tuple-element.11.poles_hbm, f32[16,8,128]{2,1,0:T(8,128)} %get-tuple-element.12.points_hbm), custom_call_target="tpu_custom_call" | custom-call | tf_op jit(solution)/shard_map/reduce/pallas_call | solution.py:600
  41.6 0.0 copy-done
  41.6 1.2 %bitcast_add_fusion = f32[256]{0:T(256)} fusion(f32[256]{0:T(256)S(1)} %copy-done, f32[2,128]{1,0:T(2,128)} %reduce.1), kind=kLoop, calls=%fused_computation | loop fusion | flops 256 | bytes 3072 | tf_op jit(solution)/shard_map/add | solution.py:619
Async XLA Ops:
  32.0 9.6 %copy-start = (f32[256]{0:T(256)S(1)}, f32[256]{0:T(256)}, u32[]{:S(2)}) copy-start(f32[256]{0:T(256)} %param.8) | copy-start | bytes 3076

commit v5 on v4

--- a/solution.py
+++ b/solution.py
@@ -36,33 +36,45 @@
 )
 
 
+def quotient(number, by):
+    return number // by if isinstance(number, int) else lax.div(number, jnp.int32(by))
+
+
+def remainder(number, by):
+    return number % by if isinstance(number, int) else lax.rem(number, jnp.int32(by))
+
+
 def block_of(place):
     kind, part = place % 4, place // 4
     return kind % 2 + (part % 2) * 2 + (kind // 2) * 4 + (part // 2) * 8
 
 
-def owner_of(place, half):
-    return (place // 8) * 16 + half * 8 + ((place // 4) % 2) * 4 + place % 4
-
-
 def stage_place(slot):
     return (slot // 8) * 8 + (slot % 2) * 4 + (slot // 2) % 4
 
 
+def far_lanes(lane):
+    side = quotient(lane, 2)
+    return 3 * (1 - side), 2 - side, side * (5 - lane) + (1 - side) * (1 - lane)
+
+
 def gather_kernel(
     plan_ref, queries_ref, triangles_ref, dipoles_ref, blocks_ref, count_ref,
-    panel_ref, poles_ref, points_ref, live_ref,
+    panel_ref, points_ref, live_ref,
     queries, triangles, dipoles, blocks, count,
-    stage, arrived, gathered, picked, late, chosen, final, message, messages, poles, live,
-    load_sems, out_sems, send_one, recv_one, send_late, recv_late, send_two, recv_two, recv_far, send_msg, recv_msg, known, go,
+    stage, gathered, picked, offered, chosen, message, messages, live,
+    load_sems, out_sems, send_one, recv_one, send_pick, recv_pick, send_two, recv_two, recv_far, send_msg, recv_msg,
 ):
     me = lax.axis_index("owner")
     lane = lax.axis_index("qgrp")
-    half = (me // 8) % 2
-    place = ((me // 16) * 2 + (me // 4) % 2) * 4 + me % 4
-    kind = me % 4
-    part = place // 4
+    kind = remainder(me, 4)
+    side = remainder(quotient(me, 4), 2)
+    half = remainder(quotient(me, 8), 2)
+    across = quotient(me, 16)
+    part = across * 2 + side
     member = kind * PAN_TURN + lane
+    squad = across * 4 + kind
+    group = me - kind
     mirror = PAN_TURN - 1 - lane
     role = half * lane + (1 - half) * mirror
     first = half == 0
@@ -83,37 +95,26 @@
     def greet(owner, to_lane):
         pl.semaphore_signal(barrier, inc=1, device_id=(owner, to_lane), device_id_type=MESH)
 
+    squads = [(dx, dk) for dx in (2, 1, 3, 0) for dk in (2, 3, 1, 0) if (dx, dk) != (0, 0)]
+    lanes = far_lanes(lane)
+
+    def comrade(dx, dk):
+        to_across, to_kind = remainder(across + dx, 4), remainder(kind + dk, 4)
+        return to_across * 4 + to_kind, (to_across * 16 + half * 8 + side * 4 + to_kind, lane)
+
     @pl.when(first)
     def _():
-        for side in range(2):
-            greet(owner_of(place - (part % 2) * 4 + side * 4, 1), mirror)
-
-        def greet_one(step, carry):
-            greet(owner_of((place + step) % BLOCKS, 0), mirror)
-            return carry
-
-        lax.fori_loop(0, BLOCKS, greet_one, 0)
-        for step in range(1, PARTS):
-            greet(owner_of(((part + step) % PARTS) * 4 + kind, 0), lane)
-        for step in range(1, 4):
-            greet((me // 4) * 4 + (me + step) % 4, lane)
-        for step in range(4):
-            greet((me // 4) * 4 + step, (lane + 2) % PAN_TURN)
-            greet((me // 4) * 4 + step, PAN_TURN - 1 - (lane + 2) % PAN_TURN)
-
-    squad = (part // 2) * 4 + kind
-
-    def comrade(step):
-        other = (squad + step) % 16
-        return other, ((other // 4) * 16 + 8 + (part % 2) * 4 + other % 4, lane)
-
-    @pl.when(jnp.logical_not(first))
-    def _():
-        def greet_comrade(step, carry):
-            greet(*comrade(step)[1])
-            return carry
-
-        lax.fori_loop(1, 16, greet_comrade, 0)
+        for to_side in range(2):
+            greet(across * 16 + 8 + to_side * 4 + kind, mirror)
+            greet(across * 16 + to_side * 4 + kind, mirror)
+
+    for dx in (2, 1, 3, 0):
+        greet(remainder(across + dx, 4) * 16 + half * 8 + (1 - side) * 4 + kind, lane)
+    for to_lane in lanes:
+        for to_kind in range(4):
+            greet(group + to_kind, to_lane)
+    for dx, dk in squads:
+        greet(*comrade(dx, dk)[1])
 
     loads[1].wait()
     flipped = jnp.concatenate(
@@ -125,109 +126,84 @@
         block = block_of(stage_place(slot))
         stage[slot // 2, slot % 2, 0:9] = triangles[:, block * BLK : (block + 1) * BLK]
         stage[slot // 2, slot % 2, 9:10, 0:8] = flipped[block : block + 1, :]
-
-    def send_first(step, carry):
-        to = (place + step) % BLOCKS
-        pltpu.make_async_remote_copy(
-            src_ref=stage.at[(to // 8) * 4 + to % 4, (to // 4) % 2], dst_ref=arrived.at[place], send_sem=send_one, recv_sem=recv_one,
-            device_id=(owner_of(to, 0), mirror), device_id_type=MESH,
-        ).start()
-        return carry
-
-    def send_comrade(step, carry):
-        other, where = comrade(step)
+    for load in loads[2:]:
+        load.wait()
+    message[0:3] = queries[:, 0:TILE]
+    message[3:6] = queries[:, TILE : 2 * TILE]
+    for tile in range(2):
+        counted = count[tile : tile + 1, :]
+        rows = [jnp.where(counted > slot, blocks[tile, slot : slot + 1, :], -1) for slot in range(NEAR)]
+        rows.append(jnp.full((1, BLK - PANELS * NEAR), -1, jnp.int32))
+        message[6 + tile : 7 + tile] = jnp.concatenate(rows, axis=1).astype(jnp.float32)
+
+    def wait_bytes(part, sem):
+        pltpu.make_async_copy(part, part, sem).wait()
+
+    pl.semaphore_wait(barrier, 15 + 4 * (PAN_TURN - 1) + 4 + 2)
+
+    for dx, dk in squads:
+        other, where = comrade(dx, dk)
         pltpu.make_async_remote_copy(
             src_ref=stage.at[other], dst_ref=gathered.at[squad], send_sem=send_one, recv_sem=recv_one,
             device_id=where, device_id_type=MESH,
         ).start()
-        return carry
-
-    def make_message():
-        for load in loads[2:]:
-            load.wait()
-        message[0:3] = queries[:, 0:TILE]
-        message[3:6] = queries[:, TILE : 2 * TILE]
-        for tile in range(2):
-            counted = count[tile : tile + 1, :]
-            rows = [jnp.where(counted > slot, blocks[tile, slot : slot + 1, :], -1) for slot in range(NEAR)]
-            rows.append(jnp.full((1, BLK - PANELS * NEAR), -1, jnp.int32))
-            message[6 + tile : 7 + tile] = jnp.concatenate(rows, axis=1).astype(jnp.float32)
-
-    def send_message(step, carry):
-        to = (member + step) % PANELS
+
+    def send_message(owner, to_lane):
         pltpu.make_async_remote_copy(
             src_ref=message, dst_ref=messages.at[member], send_sem=send_msg, recv_sem=recv_msg,
-            device_id=((me // 4) * 4 + to // PAN_TURN, to % PAN_TURN), device_id_type=MESH,
+            device_id=(owner, to_lane), device_id_type=MESH,
         ).start()
-        return carry
-
-    def send_second():
-        for step in (5, 4, 3, 6, 2, 7, 1):
-            to = ((part + step) % PARTS) * 4 + kind
-            pltpu.make_async_remote_copy(
-                src_ref=chosen, dst_ref=final.at[part], send_sem=send_two, recv_sem=recv_two,
-                device_id=(owner_of(to, half), lane), device_id_type=MESH,
-            ).start()
-
-    def wait_bytes(part, sem):
-        pltpu.make_async_copy(part, part, sem).wait()
+
+    for to_lane in lanes:
+        for to_kind in range(4):
+            send_message(group + to_kind, to_lane)
+    for dk in range(1, 4):
+        send_message(group + remainder(kind + dk, 4), lane)
+    gathered[squad] = stage[squad]
+    messages[member] = message[...]
+    wait_bytes(gathered.at[pl.ds(0, 15)], recv_one)
+    for turn in range(TURNS):
+        owner = plan_ref[turn]
+        pair = gathered[quotient(owner, 16) * 4 + remainder(owner, 4)]
+        picked[0, turn] = pair[0]
+        picked[1, turn] = pair[1]
+    for to_side in range(2):
+        pltpu.make_async_remote_copy(
+            src_ref=picked.at[to_side], dst_ref=offered.at[half * 2 + side], send_sem=send_pick, recv_sem=recv_pick,
+            device_id=(across * 16 + to_side * 4 + kind, mirror), device_id_type=MESH,
+        ).start()
 
     @pl.when(first)
     def _():
-        pl.semaphore_wait(barrier, BLOCKS + PARTS - 1 + 3 + 8)
-        lax.fori_loop(0, BLOCKS, send_first, 0)
-        make_message()
-        lax.fori_loop(1, PANELS, send_message, 0)
-        wait_bytes(arrived, recv_one)
-        wait_bytes(late, recv_late)
+        wait_bytes(offered, recv_pick)
         for turn in range(TURNS):
             owner = plan_ref[turn]
-            early = arrived[((owner // 16) * 2 + (owner // 4) % 2) * 4 + owner % 4]
-            chosen[turn] = jnp.where((owner // 8) % 2 == 0, early, late[(owner // 4) % 2, turn])
+            squad_of = remainder(quotient(owner, 8), 2) * 2 + remainder(quotient(owner, 4), 2)
+            chosen[turn] = offered[squad_of, turn]
         pltpu.make_async_remote_copy(
             src_ref=chosen, dst_ref=chosen, send_sem=send_two, recv_sem=recv_far,
             device_id=(me + 8, mirror), device_id_type=MESH,
         ).start()
-        send_second()
-        for step in range(1, PAN_TURN):
-            pl.semaphore_signal(
-                known, inc=1, device_id=(me, (lane + step) % PAN_TURN), device_id_type=MESH
-            )
-        pl.semaphore_wait(known, PAN_TURN - 1)
-        pl.semaphore_signal(go, inc=1, device_id=(me + 8, mirror), device_id_type=MESH)
 
     @pl.when(jnp.logical_not(first))
     def _():
-        pl.semaphore_wait(barrier, 15 + 2)
-        lax.fori_loop(1, 16, send_comrade, 0)
-        gathered[squad] = stage[squad]
-        wait_bytes(gathered.at[pl.ds(0, 15)], recv_one)
-        for turn in range(TURNS):
-            owner = plan_ref[turn]
-            pair = gathered[(owner // 16) * 4 + owner % 4]
-            picked[0, turn] = pair[0]
-            picked[1, turn] = pair[1]
-        for side in range(2):
-            pltpu.make_async_remote_copy(
-                src_ref=picked.at[side], dst_ref=late.at[part % 2], send_sem=send_late, recv_sem=recv_late,
-                device_id=(owner_of(place - (part % 2) * 4 + side * 4, 0), mirror), device_id_type=MESH,
-            ).start()
-        make_message()
         wait_bytes(chosen, recv_far)
-        send_second()
-        pl.semaphore_wait(go, 1)
-        lax.fori_loop(1, PANELS, send_message, 0)
-
-    final[part] = chosen[...]
-    messages[member] = message[...]
-    wait_bytes(messages.at[pl.ds(0, PANELS - 1)], recv_msg)
+
+    for dx, flip in ((2, 1), (2, 0), (1, 1), (3, 1), (0, 1), (1, 0), (3, 0)):
+        to_side = side + flip * (1 - 2 * side)
+        pltpu.make_async_remote_copy(
+            src_ref=chosen, dst_ref=panel_ref.at[part], send_sem=send_two, recv_sem=recv_two,
+            device_id=(remainder(across + dx, 4) * 16 + half * 8 + to_side * 4 + kind, lane), device_id_type=MESH,
+        ).start()
     outs = [
         pltpu.make_async_copy(source, target, out_sems.at[index])
         for index, (source, target) in enumerate(
-            [(messages, points_ref), (live, live_ref), (final, panel_ref), (poles, poles_ref)]
+            [(chosen, panel_ref.at[part]), (messages, points_ref), (live, live_ref)]
         )
     ]
     outs[0].start()
+    wait_bytes(messages.at[pl.ds(0, PANELS - 1)], recv_msg)
+    outs[1].start()
 
     shape = (PANELS, BLK)
     column = lax.broadcasted_iota(jnp.int32, shape, 1)
@@ -249,28 +225,23 @@
             one = jnp.sum(jnp.where(jnp.abs(rank - index) < 0.5, value, 0.0), axis=1, keepdims=True)
             packed = jnp.where(column == index, one, packed)
         live[:, tile, :] = packed.astype(jnp.int32)
-    outs[1].start()
-
-    wait_bytes(final.at[pl.ds(0, PARTS - 1)], recv_two)
     outs[2].start()
-    for slot in range(BLOCKS):
-        poles[slot : slot + 1] = final[slot // 4, slot % 4, 9:10, :]
-    outs[3].start()
+
+    wait_bytes(stage.at[pl.ds(0, 15)], send_one)
+    wait_bytes(picked, send_pick)
+    wait_bytes(messages.at[pl.ds(0, PANELS - 1)], send_msg)
 
     @pl.when(first)
     def _():
-        wait_bytes(stage, send_one)
-        wait_bytes(final, send_two)
+        wait_bytes(panel_ref, send_two)
 
     @pl.when(jnp.logical_not(first))
     def _():
-        wait_bytes(stage.at[pl.ds(0, 15)], send_one)
-        wait_bytes(picked, send_late)
-        wait_bytes(final.at[pl.ds(0, PARTS - 1)], send_two)
-
-    wait_bytes(messages.at[pl.ds(0, PANELS - 1)], send_msg)
+        wait_bytes(panel_ref.at[pl.ds(0, PARTS - 1)], send_two)
+
     for out in outs:
         out.wait()
+    wait_bytes(panel_ref.at[pl.ds(0, PARTS - 1)], recv_two)
 
 
 def dipole_field(centre, points):
@@ -282,7 +253,8 @@
     )
 
 
-def spread_poles(rows, centres):
+def spread_poles(poles, centres):
+    rows = jnp.concatenate([poles[slot // 4, slot % 4] for slot in range(BLOCKS)], axis=0)
     for component in range(6):
         value = jnp.broadcast_to(rows[:, component : component + 1], (BLOCKS, TILE))
         if component >= 3:
@@ -291,7 +263,7 @@
 
 
 def near_kernel(
-    live_hbm, panel_hbm, poles_hbm, points_hbm, out_ref,
+    live_hbm, panel_hbm, points_hbm, out_ref,
     live_ref, panel_ref, poles_ref, given, points_ref, flipped, picker, centres,
     spread_0, spread_1, real_0, real_1, imag_0, imag_1, turns_0, turns_1, tiles, sums, minus, sems
 ):
@@ -299,7 +271,7 @@
     loads = [
         pltpu.make_async_copy(source, target, sems.at[index])
         for index, (source, target) in enumerate(
-            [(live_hbm, live_ref), (panel_hbm, panel_ref), (poles_hbm, poles_ref), (points_hbm, given)]
+            [(live_hbm, live_ref), (panel_hbm, panel_ref), (panel_hbm.at[:, :, pl.ds(9, 1), :], poles_ref), (points_hbm, given)]
         )
     ]
     for load in loads:
@@ -310,7 +282,7 @@
     imag_0[...] = jnp.zeros_like(imag_0)
     turns_0[...] = jnp.zeros_like(turns_0)
     loads[2].wait()
-    spread_poles(poles_ref[...], centres)
+    spread_poles(poles_ref, centres)
     loads[3].wait()
     for member in range(PANELS):
         for half in range(2):
@@ -464,18 +436,18 @@
         out_ref[member] = rows[2 * member : 2 * member + 2, :]
 
 
-def near_call(live, panel, poles, points):
+def near_call(live, panel, points):
     hbm = pl.BlockSpec(memory_space=pl.ANY)
     f32 = jnp.float32
     return pl.pallas_call(
         near_kernel,
         out_shape=jax.ShapeDtypeStruct((PANELS, 2, TILE), f32),
-        in_specs=[hbm] * 4,
+        in_specs=[hbm] * 3,
         out_specs=pl.BlockSpec(memory_space=pltpu.VMEM),
         scratch_shapes=[
             pltpu.SMEM((PANELS, 2, 128), jnp.int32),
             pltpu.VMEM((PARTS, TURNS, ROWS, BLK), f32),
-            pltpu.VMEM((BLOCKS, BLK), f32),
+            pltpu.VMEM((PARTS, TURNS, 1, BLK), f32),
             pltpu.VMEM((PANELS, 8, TILE), f32),
             pltpu.VMEM((2 * PANELS, 8, TILE), f32),
             pltpu.VMEM((PANELS, TILE, 32), jnp.bfloat16),
@@ -493,39 +465,35 @@
         ],
         compiler_params=pltpu.CompilerParams(vmem_limit_bytes=60 * 1024 * 1024),
         name="near",
-    )(live, panel, poles, points)
+    )(live, panel, points)
 
 
 def reduce_kernel(
-    partial_hbm, poles_hbm, points_hbm, out_ref,
+    partial_hbm, panel_hbm, points_hbm, out_ref,
     partial, far, poles, points, centres, arrived, load_sems, send_sem, recv_sem,
 ):
     me = lax.axis_index("owner")
     lane = lax.axis_index("qgrp")
-    group = me // TURNS
-    member = (me % TURNS) * PAN_TURN + lane
+    kind = remainder(me, 4)
+    group = me - kind
+    member = kind * PAN_TURN + lane
+    partners = [(to_kind, to_lane) for to_lane in far_lanes(lane) for to_kind in range(4)]
+    partners += [(remainder(kind + dk, 4), lane) for dk in range(1, 4)]
     barrier = pltpu.get_barrier_semaphore()
     loads = [
         pltpu.make_async_copy(source, target, load_sems.at[index])
         for index, (source, target) in enumerate(
-            [(partial_hbm, partial), (poles_hbm, poles), (points_hbm, points)]
+            [(partial_hbm, partial), (panel_hbm.at[:, :, pl.ds(9, 1), :], poles), (points_hbm, points)]
         )
     ]
     for load in loads:
         load.start()
 
-    def device(step):
-        to = (member + step) % PANELS
-        return to, (group * TURNS + to // PAN_TURN, to % PAN_TURN)
-
-    def greet(step, carry):
-        pl.semaphore_signal(barrier, inc=1, device_id=device(step)[1], device_id_type=MESH)
-        return carry
-
-    lax.fori_loop(1, PANELS, greet, 0)
+    for to_kind, to_lane in partners:
+        pl.semaphore_signal(barrier, inc=1, device_id=(group + to_kind, to_lane), device_id_type=MESH)
     for load in loads:
         load.wait()
-    spread_poles(poles[...], centres)
+    spread_poles(poles, centres)
 
     def far_field(step, carry):
         for index in range(MEMBERS_STEP):
@@ -540,15 +508,11 @@
     lax.fori_loop(0, PANELS // MEMBERS_STEP, far_field, 0)
     pl.semaphore_wait(barrier, PANELS - 1)
 
-    def send(step, carry):
-        to, where = device(step)
+    for to_kind, to_lane in partners:
         pltpu.make_async_remote_copy(
-            src_ref=far.at[to], dst_ref=arrived.at[member], send_sem=send_sem, recv_sem=recv_sem,
-            device_id=where, device_id_type=MESH,
+            src_ref=far.at[to_kind * PAN_TURN + to_lane], dst_ref=arrived.at[member],
+            send_sem=send_sem, recv_sem=recv_sem, device_id=(group + to_kind, to_lane), device_id_type=MESH,
         ).start()
-        return carry
-
-    lax.fori_loop(1, PANELS, send, 0)
     arrived[member] = far[member]
     part = arrived.at[pl.ds(0, PANELS - 1)]
     pltpu.make_async_copy(part, part, recv_sem).wait()
@@ -561,42 +525,37 @@
     smem = pl.BlockSpec(memory_space=pltpu.SMEM)
     hbm = pl.BlockSpec(memory_space=pl.ANY)
     f32 = jnp.float32
-    panel, poles, points, live = pl.pallas_call(
+    panel, points, live = pl.pallas_call(
         gather_kernel,
         out_shape=(
             jax.ShapeDtypeStruct((PARTS, TURNS, ROWS, BLK), f32),
-            jax.ShapeDtypeStruct((BLOCKS, BLK), f32),
             jax.ShapeDtypeStruct((PANELS, 8, TILE), f32),
             jax.ShapeDtypeStruct((PANELS, 2, 128), jnp.int32),
         ),
         in_specs=[smem, hbm, hbm, hbm, hbm, hbm],
-        out_specs=(hbm, hbm, hbm, hbm),
+        out_specs=(hbm, hbm, hbm),
         scratch_shapes=[
             pltpu.VMEM((3, 2 * TILE), f32),
             pltpu.VMEM((9, BLOCKS * BLK), f32),
             pltpu.VMEM((6, BLOCKS), f32),
             pltpu.VMEM((2, NEAR, PANELS), jnp.int32),
             pltpu.VMEM((2, PANELS), jnp.int32),
-            pltpu.VMEM((BLOCKS // 2, 2, ROWS, BLK), f32),
-            pltpu.VMEM((BLOCKS, ROWS, BLK), f32),
-            pltpu.VMEM((BLOCKS // 2, 2, ROWS, BLK), f32),
+            pltpu.VMEM((16, 2, ROWS, BLK), f32),
+            pltpu.VMEM((16, 2, ROWS, BLK), f32),
             pltpu.VMEM((2, TURNS, ROWS, BLK), f32),
-            pltpu.VMEM((2, TURNS, ROWS, BLK), f32),
+            pltpu.VMEM((4, TURNS, ROWS, BLK), f32),
             pltpu.VMEM((TURNS, ROWS, BLK), f32),
-            pltpu.VMEM((PARTS, TURNS, ROWS, BLK), f32),
             pltpu.VMEM((8, TILE), f32),
             pltpu.VMEM((PANELS, 8, TILE), f32),
-            pltpu.VMEM((BLOCKS, BLK), f32),
             pltpu.VMEM((PANELS, 2, 128), jnp.int32),
             pltpu.SemaphoreType.DMA((5,)),
-            pltpu.SemaphoreType.DMA((4,)),
+            pltpu.SemaphoreType.DMA((3,)),
         ]
-        + [pltpu.SemaphoreType.DMA] * 9
-        + [pltpu.SemaphoreType.REGULAR] * 2,
+        + [pltpu.SemaphoreType.DMA] * 9,
         compiler_params=pltpu.CompilerParams(collective_id=0, has_side_effects=True),
         name="gather",
     )(plan, queries, triangles, dipoles, near_blocks.transpose(0, 2, 1), near_count)
-    partial = near_call(live, panel, poles, points)
+    partial = near_call(live, panel, points)
     total = pl.pallas_call(
         reduce_kernel,
         out_shape=jax.ShapeDtypeStruct((2, TILE), f32),
@@ -605,7 +564,7 @@
         scratch_shapes=[
             pltpu.VMEM((PANELS, 2, TILE), f32),
             pltpu.VMEM((PANELS, 2, TILE), f32),
-            pltpu.VMEM((BLOCKS, BLK), f32),
+            pltpu.VMEM((PARTS, TURNS, 1, BLK), f32),
             pltpu.VMEM((PANELS, 8, TILE), f32),
             pltpu.VMEM((6, BLOCKS, TILE), f32),
             pltpu.VMEM((PANELS, 2, TILE), f32),
@@ -615,7 +574,7 @@
         ],
         compiler_params=pltpu.CompilerParams(collective_id=1, has_side_effects=True),
         name="reduce",
-    )(partial, poles, points)
+    )(partial, panel, points)
     return winding_in + total.reshape(-1)
 
 

time: 43 us -> 40.9 us (0.951); the launches traced: 42.9 us -> 40.2 us
  Pallas kernels: 41.6 us -> 38.9 us
    pallas_call x1, Pallas kernels: 24.9 us -> 23.7 us  [on_device(): pl.pallas_call(gather_kernel, out_shape=(jax.ShapeDtypeStruct((PARTS, TUR...]
    pallas_call x1, Pallas kernels: 7.08 us -> 6 us  [near_call(): pl.pallas_call(near_kernel, out_shape=jax.ShapeDtypeStruct((PANELS, 2, TI...]
where the time goes in v5:
time: 40.9 us; the launch traced here: 40.2 us
  Pallas kernels  38.9 us (95%)
  other arithmetic  1.2 us (3%)
    pallas_call x1, Pallas kernels, on_device(): pl.pallas_call(gather_kernel, out_shape=(jax.ShapeDtypeStruct((PARTS, TUR...  23.7 us
    pallas_call x1, Pallas kernels, on_device(): pl.pallas_call(reduce_kernel, out_shape=jax.ShapeDtypeStruct((2, TILE), f...  9.19 us
    pallas_call x1, Pallas kernels, near_call(): pl.pallas_call(near_kernel, out_shape=jax.ShapeDtypeStruct((PANELS, 2, TI...  6 us
    add x1, other arithmetic, on_device(): return winding_in + total.reshape(-1)  1.2 us

profile of v5, /device:TPU:1, one launch (start us, length us, event | category | flops | bytes accessed | tf_op | source)
XLA Modules:
  0.0 40.2 jit_solution(11590722866049382940)
XLA Ops:
  0.0 23.7 %gather.1 = (f32[8,4,10,128]{3,2,1,0:T(8,128)}, f32[16,8,128]{2,1,0:T(8,128)}, s32[16,2,128]{2,1,0:T(2,128)}) custom-call(s32[4]{0:T(128)} %plan_ref.1, f32[3,256]{1,0:T(4,128)} %queries_ref.1, f32[9,4096]{1,0:T(8,128)} %triangles_ref.1, f32[6,32]{1,0:T(8,128)} %dipoles_ref.1, s32[2,4,16]{2,1,0:T(4,128)} %bitcast.3, s32[2,16]{1,0:T(2,128)} %count_ref.1), custom_call_target="tpu_custom_call" | custom-call | tf_op jit(solution)/shard_map/gather/pallas_call | solution.py:528
  23.7 6.0 %near.1.partial_hbm = f32[16,2,128]{2,1,0:T(2,128)} custom-call(s32[16,2,128]{2,1,0:T(2,128)} %get-tuple-element.8.live_hbm, f32[8,4,10,128]{3,2,1,0:T(8,128)} %get-tuple-element.9.panel_hbm, f32[16,8,128]{2,1,0:T(8,128)} %get-tuple-element.10.points_hbm), custom_call_target="tpu_custom_call" | custom-call | tf_op jit(solution)/shard_map/near/pallas_call | solution.py:442
  29.7 0.0 copy-start
  29.7 9.2 %reduce.1 = f32[2,128]{1,0:T(2,128)} custom-call(f32[16,2,128]{2,1,0:T(2,128)} %near.1.partial_hbm, f32[8,4,10,128]{3,2,1,0:T(8,128)} %get-tuple-element.9.panel_hbm, f32[16,8,128]{2,1,0:T(8,128)} %get-tuple-element.10.points_hbm), custom_call_target="tpu_custom_call" | custom-call | tf_op jit(solution)/shard_map/reduce/pallas_call | solution.py:559
  38.9 0.0 copy-done
  39.0 1.2 %bitcast_add_fusion = f32[256]{0:T(256)} fusion(f32[256]{0:T(256)S(1)} %copy-done, f32[2,128]{1,0:T(2,128)} %reduce.1), kind=kLoop, calls=%fused_computation | loop fusion | flops 256 | bytes 3072 | tf_op jit(solution)/shard_map/add | solution.py:578
Async XLA Ops:
  29.7 9.2 %copy-start = (f32[256]{0:T(256)S(1)}, f32[256]{0:T(256)}, u32[]{:S(2)}) copy-start(f32[256]{0:T(256)} %param.8) | copy-start | bytes 3076

commit v6 on v5

--- a/solution.py
+++ b/solution.py
@@ -18,6 +18,7 @@
 ROWS = 10
 PARTS = 8
 MEMBERS_STEP = 2
+VMEM_LIMIT = 16 * 1024 * 1024
 
 MESH = pl.DeviceIdType.MESH
 
@@ -61,7 +62,7 @@
 def gather_kernel(
     plan_ref, queries_ref, triangles_ref, dipoles_ref, blocks_ref, count_ref,
     panel_ref, points_ref, live_ref,
-    queries, triangles, dipoles, blocks, count,
+    queries, triangles, dipoles, blocks, count, turn_owner,
     stage, gathered, picked, offered, chosen, message, messages, live,
     load_sems, out_sems, send_one, recv_one, send_pick, recv_pick, send_two, recv_two, recv_far, send_msg, recv_msg,
 ):
@@ -85,7 +86,7 @@
         for index, (source, target) in enumerate(
             [
                 (triangles_ref, triangles), (dipoles_ref, dipoles), (queries_ref, queries),
-                (blocks_ref, blocks), (count_ref, count),
+                (blocks_ref, blocks), (count_ref, count), (plan_ref, turn_owner),
             ]
         )
     ]
@@ -163,7 +164,7 @@
     messages[member] = message[...]
     wait_bytes(gathered.at[pl.ds(0, 15)], recv_one)
     for turn in range(TURNS):
-        owner = plan_ref[turn]
+        owner = turn_owner[turn]
         pair = gathered[quotient(owner, 16) * 4 + remainder(owner, 4)]
         picked[0, turn] = pair[0]
         picked[1, turn] = pair[1]
@@ -177,7 +178,7 @@
     def _():
         wait_bytes(offered, recv_pick)
         for turn in range(TURNS):
-            owner = plan_ref[turn]
+            owner = turn_owner[turn]
             squad_of = remainder(quotient(owner, 8), 2) * 2 + remainder(quotient(owner, 4), 2)
             chosen[turn] = offered[squad_of, turn]
         pltpu.make_async_remote_copy(
@@ -253,8 +254,8 @@
     )
 
 
-def spread_poles(poles, centres):
-    rows = jnp.concatenate([poles[slot // 4, slot % 4] for slot in range(BLOCKS)], axis=0)
+def spread_poles(panel, centres):
+    rows = jnp.concatenate([panel[slot // 4, slot % 4, 9:10, :] for slot in range(BLOCKS)], axis=0)
     for component in range(6):
         value = jnp.broadcast_to(rows[:, component : component + 1], (BLOCKS, TILE))
         if component >= 3:
@@ -263,32 +264,23 @@
 
 
 def near_kernel(
-    live_hbm, panel_hbm, points_hbm, out_ref,
-    live_ref, panel_ref, poles_ref, given, points_ref, flipped, picker, centres,
-    spread_0, spread_1, real_0, real_1, imag_0, imag_1, turns_0, turns_1, tiles, sums, minus, sems
+    live_hbm, panel_ref, given, out_ref,
+    live_ref, points_ref, flipped, picker, centres,
+    spread_0, spread_1, real_0, real_1, imag_0, imag_1, turns_0, turns_1, tiles, sums, minus, sem
 ):
     spread, real, imag, turns = (spread_0, spread_1), (real_0, real_1), (imag_0, imag_1), (turns_0, turns_1)
-    loads = [
-        pltpu.make_async_copy(source, target, sems.at[index])
-        for index, (source, target) in enumerate(
-            [(live_hbm, live_ref), (panel_hbm, panel_ref), (panel_hbm.at[:, :, pl.ds(9, 1), :], poles_ref), (points_hbm, given)]
-        )
-    ]
-    for load in loads:
-        load.start()
+    load = pltpu.make_async_copy(live_hbm, live_ref, sem)
+    load.start()
     minus[...] = jnp.zeros_like(minus)
     sums[...] = jnp.zeros_like(sums)
     real_0[...] = jnp.ones_like(real_0)
     imag_0[...] = jnp.zeros_like(imag_0)
     turns_0[...] = jnp.zeros_like(turns_0)
-    loads[2].wait()
-    spread_poles(poles_ref, centres)
-    loads[3].wait()
+    spread_poles(panel_ref, centres)
     for member in range(PANELS):
         for half in range(2):
             points_ref[2 * member + half, 0:3] = given[member, 3 * half : 3 * half + 3]
-    loads[0].wait()
-
+    load.wait()
     tiles[0] = 2 * PANELS
     found = jnp.int32(0)
     for tile in range(2 * PANELS):
@@ -387,7 +379,6 @@
     first = widen(tiles[1])
     for part in range(TILE // 8):
         spread_part(1, part, first)
-    loads[1].wait()
 
     def one_tile(index, place):
         tile = tiles[index]
@@ -438,17 +429,15 @@
 
 def near_call(live, panel, points):
     hbm = pl.BlockSpec(memory_space=pl.ANY)
+    vmem = pl.BlockSpec(memory_space=pltpu.VMEM)
     f32 = jnp.float32
     return pl.pallas_call(
         near_kernel,
         out_shape=jax.ShapeDtypeStruct((PANELS, 2, TILE), f32),
-        in_specs=[hbm] * 3,
-        out_specs=pl.BlockSpec(memory_space=pltpu.VMEM),
+        in_specs=[hbm, vmem, vmem],
+        out_specs=vmem,
         scratch_shapes=[
             pltpu.SMEM((PANELS, 2, 128), jnp.int32),
-            pltpu.VMEM((PARTS, TURNS, ROWS, BLK), f32),
-            pltpu.VMEM((PARTS, TURNS, 1, BLK), f32),
-            pltpu.VMEM((PANELS, 8, TILE), f32),
             pltpu.VMEM((2 * PANELS, 8, TILE), f32),
             pltpu.VMEM((PANELS, TILE, 32), jnp.bfloat16),
             pltpu.VMEM((2, 32, 3 * BLK), jnp.bfloat16),
@@ -461,16 +450,15 @@
             pltpu.SMEM((2 * PANELS + 2,), jnp.int32),
             pltpu.VMEM((TILE, BLK), f32),
             pltpu.VMEM((2 * PANELS, TILE), f32),
-            pltpu.SemaphoreType.DMA((4,)),
+            pltpu.SemaphoreType.DMA,
         ],
-        compiler_params=pltpu.CompilerParams(vmem_limit_bytes=60 * 1024 * 1024),
+        compiler_params=pltpu.CompilerParams(vmem_limit_bytes=VMEM_LIMIT),
         name="near",
     )(live, panel, points)
 
 
 def reduce_kernel(
-    partial_hbm, panel_hbm, points_hbm, out_ref,
-    partial, far, poles, points, centres, arrived, load_sems, send_sem, recv_sem,
+    partial, panel, points, out_ref, far, centres, arrived, send_sem, recv_sem,
 ):
     me = lax.axis_index("owner")
     lane = lax.axis_index("qgrp")
@@ -480,20 +468,9 @@
     partners = [(to_kind, to_lane) for to_lane in far_lanes(lane) for to_kind in range(4)]
     partners += [(remainder(kind + dk, 4), lane) for dk in range(1, 4)]
     barrier = pltpu.get_barrier_semaphore()
-    loads = [
-        pltpu.make_async_copy(source, target, load_sems.at[index])
-        for index, (source, target) in enumerate(
-            [(partial_hbm, partial), (panel_hbm.at[:, :, pl.ds(9, 1), :], poles), (points_hbm, points)]
-        )
-    ]
-    for load in loads:
-        load.start()
-
     for to_kind, to_lane in partners:
         pl.semaphore_signal(barrier, inc=1, device_id=(group + to_kind, to_lane), device_id_type=MESH)
-    for load in loads:
-        load.wait()
-    spread_poles(poles, centres)
+    spread_poles(panel, centres)
 
     def far_field(step, carry):
         for index in range(MEMBERS_STEP):
@@ -522,7 +499,6 @@
 
 def on_device(queries, winding_in, triangles, dipoles, plan, near_blocks, near_count):
     vmem = pl.BlockSpec(memory_space=pltpu.VMEM)
-    smem = pl.BlockSpec(memory_space=pltpu.SMEM)
     hbm = pl.BlockSpec(memory_space=pl.ANY)
     f32 = jnp.float32
     panel, points, live = pl.pallas_call(
@@ -532,7 +508,7 @@
             jax.ShapeDtypeStruct((PANELS, 8, TILE), f32),
             jax.ShapeDtypeStruct((PANELS, 2, 128), jnp.int32),
         ),
-        in_specs=[smem, hbm, hbm, hbm, hbm, hbm],
+        in_specs=[hbm] * 6,
         out_specs=(hbm, hbm, hbm),
         scratch_shapes=[
             pltpu.VMEM((3, 2 * TILE), f32),
@@ -540,6 +516,7 @@
             pltpu.VMEM((6, BLOCKS), f32),
             pltpu.VMEM((2, NEAR, PANELS), jnp.int32),
             pltpu.VMEM((2, PANELS), jnp.int32),
+            pltpu.SMEM((TURNS,), jnp.int32),
             pltpu.VMEM((16, 2, ROWS, BLK), f32),
             pltpu.VMEM((16, 2, ROWS, BLK), f32),
             pltpu.VMEM((2, TURNS, ROWS, BLK), f32),
@@ -548,31 +525,32 @@
             pltpu.VMEM((8, TILE), f32),
             pltpu.VMEM((PANELS, 8, TILE), f32),
             pltpu.VMEM((PANELS, 2, 128), jnp.int32),
-            pltpu.SemaphoreType.DMA((5,)),
+            pltpu.SemaphoreType.DMA((6,)),
             pltpu.SemaphoreType.DMA((3,)),
         ]
         + [pltpu.SemaphoreType.DMA] * 9,
-        compiler_params=pltpu.CompilerParams(collective_id=0, has_side_effects=True),
+        compiler_params=pltpu.CompilerParams(collective_id=0, has_side_effects=True, vmem_limit_bytes=VMEM_LIMIT),
         name="gather",
-    )(plan, queries, triangles, dipoles, near_blocks.transpose(0, 2, 1), near_count)
+    )(
+        *[
+            pltpu.with_memory_space_constraint(array, pltpu.HBM)
+            for array in (plan, queries, triangles, dipoles, near_blocks.transpose(0, 2, 1), near_count)
+        ],
+    )
     partial = near_call(live, panel, points)
     total = pl.pallas_call(
         reduce_kernel,
         out_shape=jax.ShapeDtypeStruct((2, TILE), f32),
-        in_specs=[hbm] * 3,
+        in_specs=[vmem] * 3,
         out_specs=vmem,
         scratch_shapes=[
             pltpu.VMEM((PANELS, 2, TILE), f32),
-            pltpu.VMEM((PANELS, 2, TILE), f32),
-            pltpu.VMEM((PARTS, TURNS, 1, BLK), f32),
-            pltpu.VMEM((PANELS, 8, TILE), f32),
             pltpu.VMEM((6, BLOCKS, TILE), f32),
             pltpu.VMEM((PANELS, 2, TILE), f32),
-            pltpu.SemaphoreType.DMA((3,)),
             pltpu.SemaphoreType.DMA,
             pltpu.SemaphoreType.DMA,
         ],
-        compiler_params=pltpu.CompilerParams(collective_id=1, has_side_effects=True),
+        compiler_params=pltpu.CompilerParams(collective_id=1, has_side_effects=True, vmem_limit_bytes=VMEM_LIMIT),
         name="reduce",
     )(partial, panel, points)
     return winding_in + total.reshape(-1)

time: 40.9 us -> 38.6 us (0.944); the launches traced: 40.2 us -> 38.5 us
  Pallas kernels: 38.9 us -> 37.9 us
  other arithmetic: 1.2 us -> 0.57 us
    pallas_call x1, Pallas kernels: 23.7 us -> 22.9 us  [on_device(): pl.pallas_call(gather_kernel, out_shape=(jax.ShapeDtypeStruct((PARTS, TUR...]
    add x1, other arithmetic: 1.2 us -> 0.57 us  [on_device(): return winding_in + total.reshape(-1)]
    pallas_call x1, Pallas kernels: 6 us -> 5.44 us  [near_call(): pl.pallas_call(near_kernel, out_shape=jax.ShapeDtypeStruct((PANELS, 2, TI...]
where the time goes in v6:
time: 38.6 us; the launch traced here: 38.5 us
  Pallas kernels  37.9 us (98%)
  other arithmetic  0.57 us (1%)
    pallas_call x1, Pallas kernels, on_device(): pl.pallas_call(gather_kernel, out_shape=(jax.ShapeDtypeStruct((PARTS, TUR...  22.9 us
    pallas_call x1, Pallas kernels, on_device(): pl.pallas_call(reduce_kernel, out_shape=jax.ShapeDtypeStruct((2, TILE), f...  9.54 us
    pallas_call x1, Pallas kernels, near_call(): pl.pallas_call(near_kernel, out_shape=jax.ShapeDtypeStruct((PANELS, 2, TI...  5.44 us

profile of v6, /device:TPU:1, one launch (start us, length us, event | category | flops | bytes accessed | tf_op | source)
XLA Modules:
  0.0 38.5 jit_solution(15394900533965608264)
XLA Ops:
  0.0 22.9 %gather.1 = (f32[8,4,10,128]{3,2,1,0:T(8,128)S(1)}, f32[16,8,128]{2,1,0:T(8,128)S(1)}, s32[16,2,128]{2,1,0:T(2,128)S(1)}) custom-call(s32[4]{0:T(128)} %plan_ref.1, f32[3,256]{1,0:T(4,128)} %queries_ref.1, f32[9,4096]{1,0:T(8,128)} %triangles_ref.1, f32[6,32]{1,0:T(8,128)} %dipoles_ref.1, s32[2,4,16]{2,1,0:T(4,128)} %bitcast.3, s32[2,16]{1,0:T(2,128)} %count_ref.1), custom_call_target="tpu_custom_call" | custom-call | tf_op jit(solution)/shard_map/gather/pallas_call | solution.py:504
  22.9 5.4 %near.1.partial = f32[16,2,128]{2,1,0:T(2,128)S(1)} custom-call(s32[16,2,128]{2,1,0:T(2,128)S(1)} %get-tuple-element.8.live_hbm, f32[8,4,10,128]{3,2,1,0:T(8,128)S(1)} %get-tuple-element.9.panel_ref.panel, f32[16,8,128]{2,1,0:T(8,128)S(1)} %get-tuple-element.10.given.points), custom_call_target="tpu_custom_call" | custom-call | tf_op jit(solution)/shard_map/near/pallas_call | solution.py:434
  28.4 0.0 copy-start
  28.4 9.5 %reduce.1 = f32[2,128]{1,0:T(2,128)S(1)} custom-call(f32[16,2,128]{2,1,0:T(2,128)S(1)} %near.1.partial, f32[8,4,10,128]{3,2,1,0:T(8,128)S(1)} %get-tuple-element.9.panel_ref.panel, f32[16,8,128]{2,1,0:T(8,128)S(1)} %get-tuple-element.10.given.points), custom_call_target="tpu_custom_call" | custom-call | tf_op jit(solution)/shard_map/reduce/pallas_call | solution.py:541
  37.9 0.0 copy-done
  37.9 0.6 %bitcast_add_fusion = f32[256]{0:T(256)} fusion(f32[256]{0:T(256)S(1)} %copy-done, f32[2,128]{1,0:T(2,128)S(1)} %reduce.1), kind=kLoop, calls=%fused_computation | loop fusion | flops 256 | bytes 3072 | tf_op jit(solution)/shard_map/add | solution.py:556
Async XLA Ops:
  28.4 9.6 %copy-start = (f32[256]{0:T(256)S(1)}, f32[256]{0:T(256)}, u32[]{:S(2)}) copy-start(f32[256]{0:T(256)} %param.8) | copy-start | bytes 3076

commit v7 on v6

--- a/solution.py
+++ b/solution.py
@@ -16,7 +16,9 @@
 PANELS = TURNS * PAN_TURN
 OWNERS = 64
 ROWS = 10
-PARTS = 8
+MEMBERS = 8
+PARTS = 16
+HELD = PARTS * TURNS
 MEMBERS_STEP = 2
 VMEM_LIMIT = 16 * 1024 * 1024
 
@@ -61,7 +63,7 @@
 
 def gather_kernel(
     plan_ref, queries_ref, triangles_ref, dipoles_ref, blocks_ref, count_ref,
-    panel_ref, points_ref, live_ref,
+    panel_ref, points_ref, live_ref, flipped_ref,
     queries, triangles, dipoles, blocks, count, turn_owner,
     stage, gathered, picked, offered, chosen, message, messages, live,
     load_sems, out_sems, send_one, recv_one, send_pick, recv_pick, send_two, recv_two, recv_far, send_msg, recv_msg,
@@ -72,10 +74,12 @@
     side = remainder(quotient(me, 4), 2)
     half = remainder(quotient(me, 8), 2)
     across = quotient(me, 16)
-    part = across * 2 + side
-    member = kind * PAN_TURN + lane
+    core = remainder(me, 2)
+    level = remainder(quotient(me, 2), 4)
+    part = across * 4 + level
+    member = core * PAN_TURN + lane
     squad = across * 4 + kind
-    group = me - kind
+    group = me - core
     mirror = PAN_TURN - 1 - lane
     role = half * lane + (1 - half) * mirror
     first = half == 0
@@ -90,9 +94,6 @@
             ]
         )
     ]
-    for load in loads:
-        load.start()
-
     def greet(owner, to_lane):
         pl.semaphore_signal(barrier, inc=1, device_id=(owner, to_lane), device_id_type=MESH)
 
@@ -110,12 +111,16 @@
             greet(across * 16 + to_side * 4 + kind, mirror)
 
     for dx in (2, 1, 3, 0):
-        greet(remainder(across + dx, 4) * 16 + half * 8 + (1 - side) * 4 + kind, lane)
+        for low in range(2):
+            greet(remainder(across + dx, 4) * 16 + half * 8 + (1 - side) * 4 + low * 2 + core, lane)
     for to_lane in lanes:
-        for to_kind in range(4):
-            greet(group + to_kind, to_lane)
+        for to_core in range(2):
+            greet(group + to_core, to_lane)
     for dx, dk in squads:
         greet(*comrade(dx, dk)[1])
+
+    for load in loads:
+        load.start()
 
     loads[1].wait()
     flipped = jnp.concatenate(
@@ -140,7 +145,7 @@
     def wait_bytes(part, sem):
         pltpu.make_async_copy(part, part, sem).wait()
 
-    pl.semaphore_wait(barrier, 15 + 4 * (PAN_TURN - 1) + 4 + 2)
+    pl.semaphore_wait(barrier, 15 + 2 * (PAN_TURN - 1) + 8 + 2)
 
     for dx, dk in squads:
         other, where = comrade(dx, dk)
@@ -156,10 +161,9 @@
         ).start()
 
     for to_lane in lanes:
-        for to_kind in range(4):
-            send_message(group + to_kind, to_lane)
-    for dk in range(1, 4):
-        send_message(group + remainder(kind + dk, 4), lane)
+        for to_core in range(2):
+            send_message(group + to_core, to_lane)
+    send_message(group + 1 - core, lane)
     gathered[squad] = stage[squad]
     messages[member] = message[...]
     wait_bytes(gathered.at[pl.ds(0, 15)], recv_one)
@@ -190,11 +194,11 @@
     def _():
         wait_bytes(chosen, recv_far)
 
-    for dx, flip in ((2, 1), (2, 0), (1, 1), (3, 1), (0, 1), (1, 0), (3, 0)):
-        to_side = side + flip * (1 - 2 * side)
+    for dx, dy in [(dx, dy) for dx in (2, 1, 3, 0) for dy in (2, 1, 3, 0) if (dx, dy) != (0, 0)]:
+        to_level = remainder(level + dy, 4)
         pltpu.make_async_remote_copy(
             src_ref=chosen, dst_ref=panel_ref.at[part], send_sem=send_two, recv_sem=recv_two,
-            device_id=(remainder(across + dx, 4) * 16 + half * 8 + to_side * 4 + kind, lane), device_id_type=MESH,
+            device_id=(remainder(across + dx, 4) * 16 + half * 8 + to_level * 2 + core, lane), device_id_type=MESH,
         ).start()
     outs = [
         pltpu.make_async_copy(source, target, out_sems.at[index])
@@ -203,20 +207,21 @@
         )
     ]
     outs[0].start()
-    wait_bytes(messages.at[pl.ds(0, PANELS - 1)], recv_msg)
+    wait_bytes(messages.at[pl.ds(0, MEMBERS - 1)], recv_msg)
     outs[1].start()
 
-    shape = (PANELS, BLK)
+    shape = (MEMBERS, BLK)
     column = lax.broadcasted_iota(jnp.int32, shape, 1)
     before = (
         lax.broadcasted_iota(jnp.int32, (BLK, BLK), 0) < lax.broadcasted_iota(jnp.int32, (BLK, BLK), 1)
     ).astype(jnp.float32)
     for tile in range(2):
         listed = messages[:, 6 + tile, :].astype(jnp.int32)
-        held = (listed % 2) + ((listed // 4) % 2) * 2 == kind
+        held = listed % 2 == core
         held = jnp.logical_and(held, column % PAN_TURN == role)
         held = jnp.logical_and(held, jnp.logical_and(listed >= 0, column < PANELS * NEAR))
-        value = ((listed // 2) % 2 + (listed // 8) * 2) * 4 + (column % PANELS) // PAN_TURN
+        where = (listed // 8) * 4 + ((listed // 2) % 2) * 2 + (listed // 4) % 2
+        value = where * TURNS + (column % PANELS) // PAN_TURN
         value = value.astype(jnp.float32)
         flags = jnp.where(held, 1.0, 0.0)
         rank = lax.dot_general(flags, before, (((1,), (0,)), ((), ())), preferred_element_type=jnp.float32)
@@ -225,12 +230,24 @@
         for index in range(PANELS):
             one = jnp.sum(jnp.where(jnp.abs(rank - index) < 0.5, value, 0.0), axis=1, keepdims=True)
             packed = jnp.where(column == index, one, packed)
-        live[:, tile, :] = packed.astype(jnp.int32)
+        live[:, tile, :] = packed[:, 0:32].astype(jnp.int32)
     outs[2].start()
+
+    def flip(to, carry):
+        rest = messages[to]
+        parts = []
+        for _ in range(3):
+            parts.append(rest.astype(jnp.bfloat16).astype(jnp.float32))
+            rest = rest - parts[-1]
+        parts.append(jnp.zeros_like(rest))
+        flipped_ref[to] = jnp.concatenate(parts, axis=0).T.astype(jnp.bfloat16)
+        return carry
+
+    lax.fori_loop(0, MEMBERS, flip, 0)
 
     wait_bytes(stage.at[pl.ds(0, 15)], send_one)
     wait_bytes(picked, send_pick)
-    wait_bytes(messages.at[pl.ds(0, PANELS - 1)], send_msg)
+    wait_bytes(messages.at[pl.ds(0, MEMBERS - 1)], send_msg)
 
     @pl.when(first)
     def _():
@@ -255,17 +272,17 @@
 
 
 def spread_poles(panel, centres):
-    rows = jnp.concatenate([panel[slot // 4, slot % 4, 9:10, :] for slot in range(BLOCKS)], axis=0)
+    rows = jnp.concatenate([panel[slot // 4, slot % 4, 9:10, :] for slot in range(HELD)], axis=0)
     for component in range(6):
-        value = jnp.broadcast_to(rows[:, component : component + 1], (BLOCKS, TILE))
+        value = jnp.broadcast_to(rows[:, component : component + 1], (HELD, TILE))
         if component >= 3:
             value = value * (1.0 / four_pi)
         centres[component] = value
 
 
 def near_kernel(
-    live_hbm, panel_ref, given, out_ref,
-    live_ref, points_ref, flipped, picker, centres,
+    live_hbm, panel_ref, given, flipped, out_ref,
+    live_ref, points_ref, picker, centres,
     spread_0, spread_1, real_0, real_1, imag_0, imag_1, turns_0, turns_1, tiles, sums, minus, sem
 ):
     spread, real, imag, turns = (spread_0, spread_1), (real_0, real_1), (imag_0, imag_1), (turns_0, turns_1)
@@ -277,26 +294,18 @@
     imag_0[...] = jnp.zeros_like(imag_0)
     turns_0[...] = jnp.zeros_like(turns_0)
     spread_poles(panel_ref, centres)
-    for member in range(PANELS):
+    for member in range(MEMBERS):
         for half in range(2):
             points_ref[2 * member + half, 0:3] = given[member, 3 * half : 3 * half + 3]
     load.wait()
-    tiles[0] = 2 * PANELS
+    tiles[0] = 2 * MEMBERS
     found = jnp.int32(0)
-    for tile in range(2 * PANELS):
+    for tile in range(2 * MEMBERS):
         tiles[found + 1] = tile
         found = found + jnp.where(live_ref[tile // 2, tile % 2, PANELS] > 0, 1, 0)
     tiles[found + 1] = 0
     lanes = lax.broadcasted_iota(jnp.int32, (8, BLK), 1)
 
-    for member in range(PANELS):
-        rest = given[member]
-        parts = []
-        for _ in range(3):
-            parts.append(rest.astype(jnp.bfloat16).astype(jnp.float32))
-            rest = rest - parts[-1]
-        parts.append(jnp.zeros_like(rest))
-        flipped[member] = jnp.concatenate(parts, axis=0).T.astype(jnp.bfloat16)
     shape = (32, 3 * BLK)
     entry = lax.broadcasted_iota(jnp.int32, shape, 0)
     component = lax.broadcasted_iota(jnp.int32, shape, 1) // BLK
@@ -422,39 +431,38 @@
                 angle_part(place, part, tiles[found])
 
     rows = sums[...].T
-    rows = rows[0 : 2 * PANELS, :] + minus[...]
-    for member in range(PANELS):
+    rows = rows[0 : 2 * MEMBERS, :] + minus[...]
+    for member in range(MEMBERS):
         out_ref[member] = rows[2 * member : 2 * member + 2, :]
 
 
-def near_call(live, panel, points):
+def near_call(live, panel, points, flipped):
     hbm = pl.BlockSpec(memory_space=pl.ANY)
     vmem = pl.BlockSpec(memory_space=pltpu.VMEM)
     f32 = jnp.float32
     return pl.pallas_call(
         near_kernel,
-        out_shape=jax.ShapeDtypeStruct((PANELS, 2, TILE), f32),
-        in_specs=[hbm, vmem, vmem],
+        out_shape=jax.ShapeDtypeStruct((MEMBERS, 2, TILE), f32),
+        in_specs=[hbm, vmem, vmem, vmem],
         out_specs=vmem,
         scratch_shapes=[
-            pltpu.SMEM((PANELS, 2, 128), jnp.int32),
-            pltpu.VMEM((2 * PANELS, 8, TILE), f32),
-            pltpu.VMEM((PANELS, TILE, 32), jnp.bfloat16),
+            pltpu.SMEM((MEMBERS, 2, 32), jnp.int32),
+            pltpu.VMEM((2 * MEMBERS, 8, TILE), f32),
             pltpu.VMEM((2, 32, 3 * BLK), jnp.bfloat16),
-            pltpu.VMEM((6, BLOCKS, TILE), f32),
+            pltpu.VMEM((6, HELD, TILE), f32),
             pltpu.VMEM((3, TILE, BLK), f32),
             pltpu.VMEM((3, TILE, BLK), f32),
         ]
         + [pltpu.VMEM((TILE, BLK), f32)] * 6
         + [
-            pltpu.SMEM((2 * PANELS + 2,), jnp.int32),
+            pltpu.SMEM((2 * MEMBERS + 2,), jnp.int32),
             pltpu.VMEM((TILE, BLK), f32),
-            pltpu.VMEM((2 * PANELS, TILE), f32),
+            pltpu.VMEM((2 * MEMBERS, TILE), f32),
             pltpu.SemaphoreType.DMA,
         ],
         compiler_params=pltpu.CompilerParams(vmem_limit_bytes=VMEM_LIMIT),
         name="near",
-    )(live, panel, points)
+    )(live, panel, points, flipped)
 
 
 def reduce_kernel(
@@ -462,14 +470,14 @@
 ):
     me = lax.axis_index("owner")
     lane = lax.axis_index("qgrp")
-    kind = remainder(me, 4)
-    group = me - kind
-    member = kind * PAN_TURN + lane
-    partners = [(to_kind, to_lane) for to_lane in far_lanes(lane) for to_kind in range(4)]
-    partners += [(remainder(kind + dk, 4), lane) for dk in range(1, 4)]
+    core = remainder(me, 2)
+    group = me - core
+    member = core * PAN_TURN + lane
+    partners = [(to_core, to_lane) for to_lane in far_lanes(lane) for to_core in range(2)]
+    partners.append((1 - core, lane))
     barrier = pltpu.get_barrier_semaphore()
-    for to_kind, to_lane in partners:
-        pl.semaphore_signal(barrier, inc=1, device_id=(group + to_kind, to_lane), device_id_type=MESH)
+    for to_core, to_lane in partners:
+        pl.semaphore_signal(barrier, inc=1, device_id=(group + to_core, to_lane), device_id_type=MESH)
     spread_poles(panel, centres)
 
     def far_field(step, carry):
@@ -482,16 +490,16 @@
                 )
         return carry
 
-    lax.fori_loop(0, PANELS // MEMBERS_STEP, far_field, 0)
-    pl.semaphore_wait(barrier, PANELS - 1)
-
-    for to_kind, to_lane in partners:
+    lax.fori_loop(0, MEMBERS // MEMBERS_STEP, far_field, 0)
+    pl.semaphore_wait(barrier, MEMBERS - 1)
+
+    for to_core, to_lane in partners:
         pltpu.make_async_remote_copy(
-            src_ref=far.at[to_kind * PAN_TURN + to_lane], dst_ref=arrived.at[member],
-            send_sem=send_sem, recv_sem=recv_sem, device_id=(group + to_kind, to_lane), device_id_type=MESH,
+            src_ref=far.at[to_core * PAN_TURN + to_lane], dst_ref=arrived.at[member],
+            send_sem=send_sem, recv_sem=recv_sem, device_id=(group + to_core, to_lane), device_id_type=MESH,
         ).start()
     arrived[member] = far[member]
-    part = arrived.at[pl.ds(0, PANELS - 1)]
+    part = arrived.at[pl.ds(0, MEMBERS - 1)]
     pltpu.make_async_copy(part, part, recv_sem).wait()
     out_ref[...] = jnp.sum(arrived[...], axis=0)
     pltpu.make_async_copy(part, part, send_sem).wait()
@@ -501,15 +509,16 @@
     vmem = pl.BlockSpec(memory_space=pltpu.VMEM)
     hbm = pl.BlockSpec(memory_space=pl.ANY)
     f32 = jnp.float32
-    panel, points, live = pl.pallas_call(
+    panel, points, live, flipped = pl.pallas_call(
         gather_kernel,
         out_shape=(
             jax.ShapeDtypeStruct((PARTS, TURNS, ROWS, BLK), f32),
-            jax.ShapeDtypeStruct((PANELS, 8, TILE), f32),
-            jax.ShapeDtypeStruct((PANELS, 2, 128), jnp.int32),
+            jax.ShapeDtypeStruct((MEMBERS, 8, TILE), f32),
+            jax.ShapeDtypeStruct((MEMBERS, 2, 32), jnp.int32),
+            jax.ShapeDtypeStruct((MEMBERS, TILE, 32), jnp.bfloat16),
         ),
         in_specs=[hbm] * 6,
-        out_specs=(hbm, hbm, hbm),
+        out_specs=(hbm, hbm, hbm, vmem),
         scratch_shapes=[
             pltpu.VMEM((3, 2 * TILE), f32),
             pltpu.VMEM((9, BLOCKS * BLK), f32),
@@ -523,8 +532,8 @@
             pltpu.VMEM((4, TURNS, ROWS, BLK), f32),
             pltpu.VMEM((TURNS, ROWS, BLK), f32),
             pltpu.VMEM((8, TILE), f32),
-            pltpu.VMEM((PANELS, 8, TILE), f32),
-            pltpu.VMEM((PANELS, 2, 128), jnp.int32),
+            pltpu.VMEM((MEMBERS, 8, TILE), f32),
+            pltpu.VMEM((MEMBERS, 2, 32), jnp.int32),
             pltpu.SemaphoreType.DMA((6,)),
             pltpu.SemaphoreType.DMA((3,)),
         ]
@@ -537,16 +546,16 @@
             for array in (plan, queries, triangles, dipoles, near_blocks.transpose(0, 2, 1), near_count)
         ],
     )
-    partial = near_call(live, panel, points)
+    partial = near_call(live, panel, points, flipped)
     total = pl.pallas_call(
         reduce_kernel,
         out_shape=jax.ShapeDtypeStruct((2, TILE), f32),
         in_specs=[vmem] * 3,
         out_specs=vmem,
         scratch_shapes=[
-            pltpu.VMEM((PANELS, 2, TILE), f32),
-            pltpu.VMEM((6, BLOCKS, TILE), f32),
-            pltpu.VMEM((PANELS, 2, TILE), f32),
+            pltpu.VMEM((MEMBERS, 2, TILE), f32),
+            pltpu.VMEM((6, HELD, TILE), f32),
+            pltpu.VMEM((MEMBERS, 2, TILE), f32),
             pltpu.SemaphoreType.DMA,
             pltpu.SemaphoreType.DMA,
         ],

time: 38.6 us -> 38 us (0.984); the launches traced: 38.5 us -> 38.5 us
    pallas_call x1, Pallas kernels: 22.9 us -> 24.4 us  [on_device(): pl.pallas_call(gather_kernel, out_shape=(jax.ShapeDtypeStruct((PARTS, TUR...]
    pallas_call x1, Pallas kernels: 9.54 us -> 8.4 us  [on_device(): pl.pallas_call(reduce_kernel, out_shape=jax.ShapeDtypeStruct((2, TILE), f...]
where the time goes in v7:
time: 38 us; the launch traced here: 38.5 us
  Pallas kernels  37.9 us (100%)
  other arithmetic  0.57 us (1%)
    pallas_call x1, Pallas kernels, on_device(): pl.pallas_call(gather_kernel, out_shape=(jax.ShapeDtypeStruct((PARTS, TUR...  24.4 us
    pallas_call x1, Pallas kernels, on_device(): pl.pallas_call(reduce_kernel, out_shape=jax.ShapeDtypeStruct((2, TILE), f...  8.4 us
    pallas_call x1, Pallas kernels, near_call(): pl.pallas_call(near_kernel, out_shape=jax.ShapeDtypeStruct((MEMBERS, 2, T...  5.14 us

profile of v7, /device:TPU:1, one launch (start us, length us, event | category | flops | bytes accessed | tf_op | source)
XLA Modules:
  0.0 38.5 jit_solution(14846351572304279818)
XLA Ops:
  0.0 24.4 %gather.1 = (f32[16,4,10,128]{3,2,1,0:T(8,128)S(1)}, f32[8,8,128]{2,1,0:T(8,128)S(1)}, s32[8,2,32]{2,1,0:T(2,128)S(1)}, bf16[8,128,32]{2,1,0:T(8,128)(2,1)S(1)}) custom-call(s32[4]{0:T(128)} %plan_ref.1, f32[3,256]{1,0:T(4,128)} %queries_ref.1, f32[9,4096]{1,0:T(8,128)} %triangles_ref.1, f32[6,32]{1,0:T(8,128)} %dipoles_ref.1, s32[2,4,16]{2,1,0:T(4,128)} %bitcast.3, ...), custom_call_target="tpu_custom_call" | custom-call | tf_op jit(solution)/shard_map/gather/pallas_call | solution.py:512
  24.4 5.1 %near.1.partial = f32[8,2,128]{2,1,0:T(2,128)S(1)} custom-call(s32[8,2,32]{2,1,0:T(2,128)S(1)} %get-tuple-element.9.live_hbm, f32[16,4,10,128]{3,2,1,0:T(8,128)S(1)} %get-tuple-element.10.panel_ref.panel, f32[8,8,128]{2,1,0:T(8,128)S(1)} %get-tuple-element.11.given.points, bf16[8,128,32]{2,1,0:T(8,128)(2,1)S(1)} %get-tuple-element.12.flipped), custom_call_target="tpu_custom_call" | custom-call | tf_op jit(solution)/shard_map/near/pallas_call | solution.py:443
  29.5 0.0 copy-start
  29.5 8.4 %reduce.1 = f32[2,128]{1,0:T(2,128)S(1)} custom-call(f32[8,2,128]{2,1,0:T(2,128)S(1)} %near.1.partial, f32[16,4,10,128]{3,2,1,0:T(8,128)S(1)} %get-tuple-element.10.panel_ref.panel, f32[8,8,128]{2,1,0:T(8,128)S(1)} %get-tuple-element.11.given.points), custom_call_target="tpu_custom_call" | custom-call | tf_op jit(solution)/shard_map/reduce/pallas_call | solution.py:550
  37.9 0.0 copy-done
  38.0 0.6 %bitcast_add_fusion = f32[256]{0:T(256)} fusion(f32[256]{0:T(256)S(1)} %copy-done, f32[2,128]{1,0:T(2,128)S(1)} %reduce.1), kind=kLoop, calls=%fused_computation | loop fusion | flops 256 | bytes 3072 | tf_op jit(solution)/shard_map/add | solution.py:565
Async XLA Ops:
  29.5 8.4 %copy-start = (f32[256]{0:T(256)S(1)}, f32[256]{0:T(256)}, u32[]{:S(2)}) copy-start(f32[256]{0:T(256)} %param.8) | copy-start | bytes 3076

commit v8 on v7

--- a/solution.py
+++ b/solution.py
@@ -47,13 +47,8 @@
     return number % by if isinstance(number, int) else lax.rem(number, jnp.int32(by))
 
 
-def block_of(place):
-    kind, part = place % 4, place // 4
-    return kind % 2 + (part % 2) * 2 + (kind // 2) * 4 + (part // 2) * 8
-
-
-def stage_place(slot):
-    return (slot // 8) * 8 + (slot % 2) * 4 + (slot // 2) % 4
+def block_of(across, level, core):
+    return core + (level // 2) * 2 + (level % 2) * 4 + across * 8
 
 
 def far_lanes(lane):
@@ -70,15 +65,13 @@
 ):
     me = lax.axis_index("owner")
     lane = lax.axis_index("qgrp")
-    kind = remainder(me, 4)
-    side = remainder(quotient(me, 4), 2)
     half = remainder(quotient(me, 8), 2)
     across = quotient(me, 16)
     core = remainder(me, 2)
     level = remainder(quotient(me, 2), 4)
     part = across * 4 + level
     member = core * PAN_TURN + lane
-    squad = across * 4 + kind
+    squad = across * 2 + core
     group = me - core
     mirror = PAN_TURN - 1 - lane
     role = half * lane + (1 - half) * mirror
@@ -97,27 +90,27 @@
     def greet(owner, to_lane):
         pl.semaphore_signal(barrier, inc=1, device_id=(owner, to_lane), device_id_type=MESH)
 
-    squads = [(dx, dk) for dx in (2, 1, 3, 0) for dk in (2, 3, 1, 0) if (dx, dk) != (0, 0)]
+    squads = [(dx, dc) for dx in (2, 1, 3, 0) for dc in (1, 0) if (dx, dc) != (0, 0)]
     lanes = far_lanes(lane)
 
-    def comrade(dx, dk):
-        to_across, to_kind = remainder(across + dx, 4), remainder(kind + dk, 4)
-        return to_across * 4 + to_kind, (to_across * 16 + half * 8 + side * 4 + to_kind, lane)
+    def comrade(dx, dc):
+        to_across, to_core = remainder(across + dx, 4), remainder(core + dc, 2)
+        return to_across * 2 + to_core, (to_across * 16 + half * 8 + level * 2 + to_core, lane)
 
     @pl.when(first)
     def _():
-        for to_side in range(2):
-            greet(across * 16 + 8 + to_side * 4 + kind, mirror)
-            greet(across * 16 + to_side * 4 + kind, mirror)
+        for to_level in range(4):
+            greet(across * 16 + 8 + to_level * 2 + core, mirror)
+            greet(across * 16 + to_level * 2 + core, mirror)
 
     for dx in (2, 1, 3, 0):
-        for low in range(2):
-            greet(remainder(across + dx, 4) * 16 + half * 8 + (1 - side) * 4 + low * 2 + core, lane)
+        for dy in (2, 1, 3):
+            greet(remainder(across + dx, 4) * 16 + half * 8 + remainder(level + dy, 4) * 2 + core, lane)
     for to_lane in lanes:
         for to_core in range(2):
             greet(group + to_core, to_lane)
-    for dx, dk in squads:
-        greet(*comrade(dx, dk)[1])
+    for dx, dc in squads:
+        greet(*comrade(dx, dc)[1])
 
     for load in loads:
         load.start()
@@ -129,9 +122,9 @@
     ).T
     loads[0].wait()
     for slot in range(BLOCKS):
-        block = block_of(stage_place(slot))
-        stage[slot // 2, slot % 2, 0:9] = triangles[:, block * BLK : (block + 1) * BLK]
-        stage[slot // 2, slot % 2, 9:10, 0:8] = flipped[block : block + 1, :]
+        block = block_of(slot // 8, slot % 4, (slot // 4) % 2)
+        stage[slot // 4, slot % 4, 0:9] = triangles[:, block * BLK : (block + 1) * BLK]
+        stage[slot // 4, slot % 4, 9:10, 0:8] = flipped[block : block + 1, :]
     for load in loads[2:]:
         load.wait()
     message[0:3] = queries[:, 0:TILE]
@@ -145,10 +138,10 @@
     def wait_bytes(part, sem):
         pltpu.make_async_copy(part, part, sem).wait()
 
-    pl.semaphore_wait(barrier, 15 + 2 * (PAN_TURN - 1) + 8 + 2)
-
-    for dx, dk in squads:
-        other, where = comrade(dx, dk)
+    pl.semaphore_wait(barrier, 7 + 2 * (PAN_TURN - 1) + 12 + 4)
+
+    for dx, dc in squads:
+        other, where = comrade(dx, dc)
         pltpu.make_async_remote_copy(
             src_ref=stage.at[other], dst_ref=gathered.at[squad], send_sem=send_one, recv_sem=recv_one,
             device_id=where, device_id_type=MESH,
@@ -166,16 +159,17 @@
     send_message(group + 1 - core, lane)
     gathered[squad] = stage[squad]
     messages[member] = message[...]
-    wait_bytes(gathered.at[pl.ds(0, 15)], recv_one)
+    wait_bytes(gathered.at[pl.ds(0, 7)], recv_one)
     for turn in range(TURNS):
         owner = turn_owner[turn]
-        pair = gathered[quotient(owner, 16) * 4 + remainder(owner, 4)]
-        picked[0, turn] = pair[0]
-        picked[1, turn] = pair[1]
-    for to_side in range(2):
+        pieces = gathered[quotient(owner, 16) * 2 + remainder(owner, 2)]
+        for to_level in range(4):
+            picked[to_level, turn] = pieces[to_level]
+    for dy in (2, 1, 3, 0):
+        to_level = remainder(level + dy, 4)
         pltpu.make_async_remote_copy(
-            src_ref=picked.at[to_side], dst_ref=offered.at[half * 2 + side], send_sem=send_pick, recv_sem=recv_pick,
-            device_id=(across * 16 + to_side * 4 + kind, mirror), device_id_type=MESH,
+            src_ref=picked.at[to_level], dst_ref=offered.at[half * 4 + level], send_sem=send_pick, recv_sem=recv_pick,
+            device_id=(across * 16 + to_level * 2 + core, mirror), device_id_type=MESH,
         ).start()
 
     @pl.when(first)
@@ -183,7 +177,7 @@
         wait_bytes(offered, recv_pick)
         for turn in range(TURNS):
             owner = turn_owner[turn]
-            squad_of = remainder(quotient(owner, 8), 2) * 2 + remainder(quotient(owner, 4), 2)
+            squad_of = remainder(quotient(owner, 8), 2) * 4 + remainder(quotient(owner, 2), 4)
             chosen[turn] = offered[squad_of, turn]
         pltpu.make_async_remote_copy(
             src_ref=chosen, dst_ref=chosen, send_sem=send_two, recv_sem=recv_far,
@@ -245,7 +239,7 @@
 
     lax.fori_loop(0, MEMBERS, flip, 0)
 
-    wait_bytes(stage.at[pl.ds(0, 15)], send_one)
+    wait_bytes(stage.at[pl.ds(0, 7)], send_one)
     wait_bytes(picked, send_pick)
     wait_bytes(messages.at[pl.ds(0, MEMBERS - 1)], send_msg)
 
@@ -526,10 +520,10 @@
             pltpu.VMEM((2, NEAR, PANELS), jnp.int32),
             pltpu.VMEM((2, PANELS), jnp.int32),
             pltpu.SMEM((TURNS,), jnp.int32),
-            pltpu.VMEM((16, 2, ROWS, BLK), f32),
-            pltpu.VMEM((16, 2, ROWS, BLK), f32),
-            pltpu.VMEM((2, TURNS, ROWS, BLK), f32),
+            pltpu.VMEM((8, 4, ROWS, BLK), f32),
+            pltpu.VMEM((8, 4, ROWS, BLK), f32),
             pltpu.VMEM((4, TURNS, ROWS, BLK), f32),
+            pltpu.VMEM((8, TURNS, ROWS, BLK), f32),
             pltpu.VMEM((TURNS, ROWS, BLK), f32),
             pltpu.VMEM((8, TILE), f32),
             pltpu.VMEM((MEMBERS, 8, TILE), f32),

time: 38 us -> 38.2 us (level); the launches traced: 38.5 us -> 37.7 us
  Pallas kernels: 37.9 us -> 37.1 us
    pallas_call x1, Pallas kernels: 5.14 us -> 3.57 us  [near_call(): pl.pallas_call(near_kernel, out_shape=jax.ShapeDtypeStruct((MEMBERS, 2, T...]
    pallas_call x1, Pallas kernels: 24.4 us -> 25.7 us  [on_device(): pl.pallas_call(gather_kernel, out_shape=(jax.ShapeDtypeStruct((PARTS, TUR...]
    pallas_call x1, Pallas kernels: 8.4 us -> 7.82 us  [on_device(): pl.pallas_call(reduce_kernel, out_shape=jax.ShapeDtypeStruct((2, TILE), f...]
where the time goes in v8:
time: 38.2 us; the launch traced here: 37.7 us
  Pallas kernels  37.1 us (97%)
  other arithmetic  0.57 us (1%)
    pallas_call x1, Pallas kernels, on_device(): pl.pallas_call(gather_kernel, out_shape=(jax.ShapeDtypeStruct((PARTS, TUR...  25.7 us
    pallas_call x1, Pallas kernels, on_device(): pl.pallas_call(reduce_kernel, out_shape=jax.ShapeDtypeStruct((2, TILE), f...  7.82 us
    pallas_call x1, Pallas kernels, near_call(): pl.pallas_call(near_kernel, out_shape=jax.ShapeDtypeStruct((MEMBERS, 2, T...  3.57 us

profile of v8, /device:TPU:1, one launch (start us, length us, event | category | flops | bytes accessed | tf_op | source)
XLA Modules:
  0.0 37.7 jit_solution(10896196802917803201)
XLA Ops:
  0.0 25.7 %gather.1 = (f32[16,4,10,128]{3,2,1,0:T(8,128)S(1)}, f32[8,8,128]{2,1,0:T(8,128)S(1)}, s32[8,2,32]{2,1,0:T(2,128)S(1)}, bf16[8,128,32]{2,1,0:T(8,128)(2,1)S(1)}) custom-call(s32[4]{0:T(128)} %plan_ref.1, f32[3,256]{1,0:T(4,128)} %queries_ref.1, f32[9,4096]{1,0:T(8,128)} %triangles_ref.1, f32[6,32]{1,0:T(8,128)} %dipoles_ref.1, s32[2,4,16]{2,1,0:T(4,128)} %bitcast.3, ...), custom_call_target="tpu_custom_call" | custom-call | tf_op jit(solution)/shard_map/gather/pallas_call | solution.py:506
  25.7 3.6 %near.1.partial = f32[8,2,128]{2,1,0:T(2,128)S(1)} custom-call(s32[8,2,32]{2,1,0:T(2,128)S(1)} %get-tuple-element.9.live_hbm, f32[16,4,10,128]{3,2,1,0:T(8,128)S(1)} %get-tuple-element.10.panel_ref.panel, f32[8,8,128]{2,1,0:T(8,128)S(1)} %get-tuple-element.11.given.points, bf16[8,128,32]{2,1,0:T(8,128)(2,1)S(1)} %get-tuple-element.12.flipped), custom_call_target="tpu_custom_call" | custom-call | tf_op jit(solution)/shard_map/near/pallas_call | solution.py:437
  29.3 0.0 copy-start
  29.3 7.8 %reduce.1 = f32[2,128]{1,0:T(2,128)S(1)} custom-call(f32[8,2,128]{2,1,0:T(2,128)S(1)} %near.1.partial, f32[16,4,10,128]{3,2,1,0:T(8,128)S(1)} %get-tuple-element.10.panel_ref.panel, f32[8,8,128]{2,1,0:T(8,128)S(1)} %get-tuple-element.11.given.points), custom_call_target="tpu_custom_call" | custom-call | tf_op jit(solution)/shard_map/reduce/pallas_call | solution.py:544
  37.1 0.0 copy-done
  37.1 0.6 %bitcast_add_fusion = f32[256]{0:T(256)} fusion(f32[256]{0:T(256)S(1)} %copy-done, f32[2,128]{1,0:T(2,128)S(1)} %reduce.1), kind=kLoop, calls=%fused_computation | loop fusion | flops 256 | bytes 3072 | tf_op jit(solution)/shard_map/add | solution.py:559
Async XLA Ops:
  29.3 7.8 %copy-start = (f32[256]{0:T(256)S(1)}, f32[256]{0:T(256)}, u32[]{:S(2)}) copy-start(f32[256]{0:T(256)} %param.8) | copy-start | bytes 3076
